TPU v7x, 32 devices: a whole 2x2x4 slice. The times are simulated.
32 devices in a mesh: tile: 16 (over z, x, core), tm: 2 (over y).
Axes of the slice: x: 2, y: 2, z: 4, core: 2. Of those that a mesh axis runs over, the one named last changes fastest.
Arguments:
- features: bfloat16 [192, 8, 16, 16, 128], P('tile', 'tm'), may hold values from -6 to 6
- weight_one: bfloat16 [3, 3, 128, 128], replicated, may hold values from -0.1875 to 0.1875
- bias_one: float32 [128], replicated, may hold values from -3 to 3
- weight_two: bfloat16 [3, 3, 128, 128], replicated, may hold values from -0.1875 to 0.1875
- bias_two: float32 [128], replicated, may hold values from -3 to 3
- cotangent: bfloat16 [192, 8, 16, 16, 128], P('tile', 'tm'), may hold values from -6 to 6
Outputs:
- output: bfloat16 [192, 8, 16, 16, 128], P('tile', 'tm')
- grad_weight_one: float32 [3, 3, 128, 128], replicated
- grad_bias_one: float32 [128], replicated
- grad_weight_two: float32 [3, 3, 128, 128], replicated
- grad_bias_two: float32 [128], replicated
All inputs are finite; a program needn't handle non-finite values.
Results may differ from a plain program's by a relative error of at most 0.0085.
Values may be sent and summed in bfloat16 or wider, within the bound.
A program may use at most 256 MiB of HBM per device.

v0:
```python
import math

import jax
import jax.numpy as jnp
import numpy as np
from jax import lax
from jax.experimental import pallas as pl
from jax.experimental.pallas import tpu as pltpu
from jax.sharding import PartitionSpec as P

S = 4


inv_sqrt_two = 0.7071067811865476
inv_sqrt_tau = 0.3989422804014327


def passed_along(value, axis, steps):
    count = lax.axis_size(axis)
    pairs = [(source, (source + steps) % count) for source in range(count)]
    return lax.ppermute(value, axis, pairs)


def edge_partner(face_id, edge_id):
    group_id = face_id // 4
    within = face_id % 4
    after_id = (within + 1) % 4
    before = (within + 3) % 4
    if group_id == 0:
        options = [(after_id, 2), (4 + within, 0), (before, 0), (4 + after_id, 2)]
    elif group_id == 1:
        options = [(within, 1), (8 + before, 0), (before, 3), (8 + within, 2)]
    else:
        options = [(4 + after_id, 1), (8 + before, 3), (4 + within, 3), (8 + after_id, 1)]
    return options[edge_id]


def entry_pixel(edge_id, along_edge, length):
    if edge_id == 0:
        return (0, along_edge)
    if edge_id == 1:
        return (length - 1, along_edge)
    if edge_id == 2:
        return (along_edge, 0)
    return (along_edge, length - 1)


def step_pixel(face_id, row_at, col_at, row_step, col_step, length):
    row_new = row_at + row_step
    col_new = col_at + col_step
    if 0 <= row_new < length and 0 <= col_new < length:
        return (face_id, row_new, col_new, -1)
    if row_new < 0:
        edge_id = 0
    elif row_new >= length:
        edge_id = 1
    elif col_new < 0:
        edge_id = 2
    else:
        edge_id = 3
    along_edge = col_at if edge_id < 2 else row_at
    partner, entered = edge_partner(face_id, edge_id)
    row_in, col_in = entry_pixel(entered, along_edge, length)
    return (partner, row_in, col_in, entered)


def neighbour_pixel(face_id, row_at, col_at, row_step, col_step, length):
    if row_step == 0 or col_step == 0:
        found = step_pixel(face_id, row_at, col_at, row_step, col_step, length)
        return (found[0], found[1], found[2])
    face_one, row_one, col_one, entered = step_pixel(face_id, row_at, col_at, row_step, 0, length)
    if entered >= 2:
        found = step_pixel(face_one, row_one, col_one, col_step, 0, length)
    else:
        found = step_pixel(face_one, row_one, col_one, 0, col_step, length)
    return (found[0], found[1], found[2])


def tile_slot(face_id, tile_row, tile_col, side_tiles):
    group_id = face_id // 4
    within = face_id % 4
    extra = 1 if group_id == 2 else 0
    column = (side_tiles * (within + extra) + tile_col) % (4 * side_tiles)
    return 3 * side_tiles * column + side_tiles * group_id + tile_row


def cycle_position(row_at, col_at, pixels):
    if row_at == 0:
        return col_at
    if row_at == pixels - 1:
        return pixels + col_at
    if col_at == 0:
        return 2 * pixels + row_at
    return 3 * pixels + row_at


def halo_positions(pixels):
    places = [(-1, column) for column in range(-1, pixels + 1)]
    places = places + [(pixels, column) for column in range(-1, pixels + 1)]
    places = places + [(row_at, -1) for row_at in range(pixels)]
    places = places + [(row_at, pixels) for row_at in range(pixels)]
    return places


def halo_sources(side_tiles, pixels):
    slot_count = 12 * side_tiles * side_tiles
    places = halo_positions(pixels)
    length = side_tiles * pixels
    source_slot = np.zeros((slot_count, len(places)), np.int64)
    source_cycle = np.zeros((slot_count, len(places)), np.int64)
    for face_id in range(12):
        for tile_row in range(side_tiles):
            for tile_col in range(side_tiles):
                slot_id = tile_slot(face_id, tile_row, tile_col, side_tiles)
                for cell_index in range(len(places)):
                    row_at, col_at = places[cell_index]
                    inner_row = min(max(row_at, 0), pixels - 1)
                    inner_col = min(max(col_at, 0), pixels - 1)
                    partner, row_new, col_new = neighbour_pixel(
                        face_id,
                        tile_row * pixels + inner_row,
                        tile_col * pixels + inner_col,
                        row_at - inner_row,
                        col_at - inner_col,
                        length,
                    )
                    source_slot[slot_id, cell_index] = tile_slot(
                        partner, row_new // pixels, col_new // pixels, side_tiles
                    )
                    source_cycle[slot_id, cell_index] = cycle_position(
                        row_new % pixels, col_new % pixels, pixels
                    )
    return (source_slot, source_cycle)


def halo_rows(row_at, col_at, pixels):
    if row_at == -1 or row_at == pixels:
        base = 0 if row_at == -1 else 3 * pixels
        return [
            base + pixels * shift + col_at + 1 - shift
            for shift in range(3)
            if 0 <= col_at + 1 - shift < pixels
        ]
    return [6 * pixels + row_at if col_at == -1 else 7 * pixels + row_at]


def outer_row(row_at, col_at, pixels):
    if col_at == -1:
        return 2 * pixels + row_at + 1
    if col_at == pixels:
        return 4 * pixels + row_at + 1
    return col_at if row_at == -1 else pixels + col_at


def device_tables(device_count, per_device, side_tiles, pixels):
    source_slot, source_cycle = halo_sources(side_tiles, pixels)
    places = halo_positions(pixels)
    rim_len, halo_len, outer_len = 4 * pixels, 8 * pixels, 6 * pixels
    sends = {}
    local = []
    for device in range(device_count):
        local.append([])
        for local_id in range(per_device):
            slot_id = device * per_device + local_id
            for cell in range(len(places)):
                row_at, col_at = places[cell]
                source = int(source_slot[slot_id, cell])
                moved_by = (device - source // per_device) % device_count
                if moved_by > device_count // 2:
                    moved_by -= device_count
                rim = source % per_device * rim_len + int(source_cycle[slot_id, cell])
                halo = [local_id * halo_len + h for h in halo_rows(row_at, col_at, pixels)]
                outer = local_id * outer_len + outer_row(row_at, col_at, pixels)
                record = (rim, halo, outer)
                if moved_by == 0:
                    local[device].append(record)
                else:
                    lists = sends.setdefault(moved_by, [[] for _ in range(device_count)])
                    lists[device].append(record)
    offsets = sorted(sends)
    widths = [-(-max(len(one) for one in sends[offset]) // 16) * 16 for offset in offsets]
    total = sum(widths)
    send = np.full((device_count, total), -1, np.int32)
    receive = np.full((device_count, per_device * halo_len), -1, np.int32)
    back = np.full((device_count, total), -1, np.int32)
    target = np.full((device_count, per_device * outer_len + total), -1, np.int32)
    for device in range(device_count):
        for rim, halo, outer in local[device]:
            receive[device, halo] = rim
            target[device, outer] = rim
        base = 0
        for offset, width in zip(offsets, widths):
            sender = (device - offset) % device_count
            for at, (rim, halo, outer) in enumerate(sends[offset][device]):
                send[sender, base + at] = rim
                receive[device, halo] = per_device * rim_len + base + at
                back[device, base + at] = outer
                target[sender, per_device * outer_len + base + at] = rim
            base += width
    return (offsets, widths, send, receive, back, target)


def one_hot(table_np, tile_index, width):
    row = jnp.asarray(table_np, dtype=jnp.int32)[tile_index]
    return (row[:, None] == lax.broadcasted_iota(jnp.int32, (row.shape[0], width), 1)).astype(
        jnp.bfloat16
    )


def exchanged(rows, offsets, widths, sign):
    pieces, base = [], 0
    for offset, width in zip(offsets, widths):
        pieces.append(passed_along(rows[base : base + width], "tile", sign * offset))
        base += width
    return pieces


def halo_of(rim, layout, tile_index):
    offsets, widths, send, receive = layout[:4]
    outgoing = jnp.dot(one_hot(send, tile_index, rim.shape[0]), rim)
    pool = jnp.concatenate([rim] + exchanged(outgoing, offsets, widths, 1), axis=0)
    return jnp.dot(one_hot(receive, tile_index, pool.shape[0]), pool)


def folded(outer, layout, tile_index, rim_rows):
    offsets, widths, _, _, back, target = layout
    outgoing = jnp.dot(one_hot(back, tile_index, outer.shape[0]), outer)
    pool = jnp.concatenate([outer] + exchanged(outgoing, offsets, widths, -1), axis=0)
    spread = one_hot(target, tile_index, rim_rows)
    return lax.dot_general(
        spread, pool, (((0,), (0,)), ((), ())), preferred_element_type=jnp.float32
    )


def gelu_parts(value):
    half = 0.5 * (1.0 + lax.erf(value * inv_sqrt_two))
    return value * half, half + value * jnp.exp(-0.5 * value * value) * inv_sqrt_tau


def columns_at(tile, halo, work, pixels):
    count = pixels * pixels
    wide = tile.astype(jnp.float32)
    halo_wide = halo[6 * pixels :].astype(jnp.float32)
    work[0, pl.ds(1, count - 1), :] = wide[: count - 1]
    work[0, pl.ds(0, pixels, stride=pixels), :] = halo_wide[:pixels]
    work[1, pl.ds(0, count - 1), :] = wide[1:]
    work[1, pl.ds(pixels - 1, pixels, stride=pixels), :] = halo_wide[pixels:]
    middles = [work[0].astype(jnp.bfloat16), tile, work[1].astype(jnp.bfloat16)]
    joined = jnp.concatenate(
        [
            jnp.concatenate(
                [
                    halo[pixels * b : pixels * (b + 1)],
                    middles[b],
                    halo[pixels * (3 + b) : pixels * (4 + b)],
                ],
                axis=0,
            )
            for b in range(3)
        ],
        axis=1,
    )
    return jnp.concatenate([joined[pixels * a : pixels * a + count] for a in range(3)], axis=1)


def first_kernel(x_ref, halo_ref, w_ref, bias_ref, hidden_ref, slope_ref, rim_ref, work):
    batch, pixels, channels = x_ref.shape[1], x_ref.shape[2], x_ref.shape[4]
    count = pixels * pixels
    for s in range(batch):
        lanes = slice(s * channels, (s + 1) * channels)
        tile = x_ref[0, s].reshape(count, channels)
        cols = columns_at(tile, halo_ref[0, :, lanes], work.at[pl.ds(2 * s, 2)], pixels)
        pre = jnp.dot(cols, w_ref[...], preferred_element_type=jnp.float32) + bias_ref[...]
        hidden, slope = gelu_parts(pre)
        slope_ref[0, s] = slope
        work[2 * batch + s] = hidden
        rounded = hidden.astype(jnp.bfloat16)
        hidden_ref[0, s] = rounded.reshape(pixels, pixels, channels)
        rim_ref[0, 0:pixels, lanes] = rounded[:pixels]
        rim_ref[0, pixels : 2 * pixels, lanes] = rounded[count - pixels :]
        for side in range(2):
            edge = work[2 * batch + s, pl.ds(side * (pixels - 1), pixels, stride=pixels), :]
            rim_ref[0, (2 + side) * pixels : (3 + side) * pixels, lanes] = edge.astype(jnp.bfloat16)


def second_kernel(
    x_ref, halo_ref, cot_ref, w_ref, flip_ref, side_ref, bias_ref,
    out_ref, inner_ref, outer_ref, grad_ref, sum_ref, work, cols_ref, delta_ref, edge_ref,
):
    batch, pixels, channels = x_ref.shape[1], x_ref.shape[2], x_ref.shape[4]
    count = pixels * pixels

    @pl.when(pl.program_id(0) == 0)
    def _():
        grad_ref[...] = jnp.zeros_like(grad_ref)
        sum_ref[...] = jnp.zeros_like(sum_ref)

    zero_row = jnp.zeros((1, channels), jnp.float32)
    zero_col = jnp.zeros((pixels, channels), jnp.float32)
    zeros = jnp.zeros((2 * pixels, 3 * channels), jnp.bfloat16)
    for s in range(batch):
        lanes = slice(s * channels, (s + 1) * channels)
        tile = x_ref[0, s].reshape(count, channels)
        here = work.at[pl.ds(2 * s, 2)]
        cols = columns_at(tile, halo_ref[0, :, lanes], here, pixels)
        cols_ref[s * count : (s + 1) * count, :] = cols
        pre = jnp.dot(cols, w_ref[...], preferred_element_type=jnp.float32) + bias_ref[...]
        value, slope = gelu_parts(pre)
        out_ref[0, s] = value.astype(jnp.bfloat16).reshape(pixels, pixels, channels)
        cot = cot_ref[0, s].reshape(count, channels).astype(jnp.float32)
        delta = (cot * slope).astype(jnp.bfloat16)
        delta_ref[s * count : (s + 1) * count, :] = delta
        wide = delta.astype(jnp.float32)
        sum_ref[...] += jnp.sum(wide, axis=0, keepdims=True)
        edge_ref[s] = jnp.zeros(edge_ref.shape[1:], jnp.float32)
        work[2 * batch + s] = wide
        for side in range(2):
            edge_ref[s, side, pl.ds(2, pixels), :] = work[
                2 * batch + s, pl.ds(side * (pixels - 1), pixels, stride=pixels), :
            ]
        here[0, pl.ds(0, count - 1), :] = wide[1:]
        here[0, pl.ds(pixels - 1, pixels, stride=pixels), :] = zero_col
        here[1, pl.ds(1, count - 1), :] = wide[: count - 1]
        here[1, pl.ds(0, pixels, stride=pixels), :] = zero_col
        joined = jnp.concatenate(
            [here[0].astype(jnp.bfloat16), delta, here[1].astype(jnp.bfloat16)], axis=1
        )
        joined = jnp.concatenate([zeros, joined, zeros], axis=0)
        tall = count + 2 * pixels
        spread = jnp.concatenate(
            [joined[pixels * (2 - a) : pixels * (2 - a) + tall] for a in range(3)], axis=1
        )
        grad = jnp.dot(spread, flip_ref[...], preferred_element_type=jnp.float32)
        inner_ref[0, s] = grad[pixels : pixels + count]
        outer_ref[0, 0:pixels, lanes] = grad[:pixels].astype(jnp.bfloat16)
        outer_ref[0, pixels : 2 * pixels, lanes] = grad[pixels + count :].astype(jnp.bfloat16)
        for side in range(2):
            lhs = jnp.concatenate(
                [edge_ref[s, side, pl.ds(2 - a, 2 * pixels), :] for a in range(3)], axis=1
            ).astype(jnp.bfloat16)
            part = jnp.dot(lhs, side_ref[side], preferred_element_type=jnp.float32)
            outer_ref[0, 2 * pixels * (1 + side) : 2 * pixels * (2 + side), lanes] = part.astype(
                jnp.bfloat16
            )
    grad_ref[...] += lax.dot_general(
        delta_ref[...], cols_ref[...], (((0,), (0,)), ((), ())), preferred_element_type=jnp.float32
    )


def third_kernel(
    x_ref, halo_ref, inner_ref, rim_ref, slope_ref, grad_ref, sum_ref, work, cols_ref, delta_ref
):
    batch, pixels, channels = x_ref.shape[1], x_ref.shape[2], x_ref.shape[4]
    count = pixels * pixels

    @pl.when(pl.program_id(0) == 0)
    def _():
        grad_ref[...] = jnp.zeros_like(grad_ref)
        sum_ref[...] = jnp.zeros_like(sum_ref)

    for s in range(batch):
        lanes = slice(s * channels, (s + 1) * channels)
        tile = x_ref[0, s].reshape(count, channels)
        cols_ref[s * count : (s + 1) * count, :] = columns_at(
            tile, halo_ref[0, :, lanes], work.at[pl.ds(2 * s, 2)], pixels
        )
        at = 2 * batch + s
        work[at] = inner_ref[0, s]
        work[at, pl.ds(0, pixels), :] += rim_ref[0, 0:pixels, lanes]
        work[at, pl.ds(count - pixels, pixels), :] += rim_ref[0, pixels : 2 * pixels, lanes]
        for side in range(2):
            place = pl.ds(side * (pixels - 1), pixels, stride=pixels)
            edge = rim_ref[0, (2 + side) * pixels : (3 + side) * pixels, lanes]
            work[at, place, :] = work[at, place, :] + edge
        delta = (work[at] * slope_ref[0, s]).astype(jnp.bfloat16)
        delta_ref[s * count : (s + 1) * count, :] = delta
        sum_ref[...] += jnp.sum(delta.astype(jnp.float32), axis=0, keepdims=True)
    grad_ref[...] += lax.dot_general(
        delta_ref[...], cols_ref[...], (((0,), (0,)), ((), ())), preferred_element_type=jnp.float32
    )


def per_tile(shape):
    return pl.BlockSpec((1,) + tuple(shape), lambda t: (t,) + (0,) * len(shape))


def whole(shape):
    return pl.BlockSpec(tuple(shape), lambda t: (0,) * len(shape))


params = dict(vmem_limit_bytes=48 * 1024 * 1024)


def body(features, weight_one, bias_one, weight_two, bias_two, cotangent):
    device_count = lax.axis_size("tile")
    samples_count = lax.axis_size("tm")
    tile_index = lax.axis_index("tile")
    per_device, batch, pixels, _, channels = features.shape
    count = pixels * pixels
    lane_count = batch * channels
    layout = device_tables(device_count, per_device, S, pixels)
    bf16, f32 = jnp.bfloat16, jnp.float32
    tile_shape = (batch, pixels, pixels, channels)
    flat_shape = (batch, count, channels)
    halo_shape = (8 * pixels, lane_count)
    rim_shape = (4 * pixels, lane_count)
    outer_shape = (6 * pixels, lane_count)
    mat_one = weight_one.reshape(9 * channels, channels)
    mat_two = weight_two.reshape(9 * channels, channels)
    turned = weight_two.transpose(0, 1, 3, 2)
    flip = turned.reshape(9 * channels, channels)
    sides = jnp.stack([turned[:, 0], turned[:, 2]]).reshape(2, 3 * channels, channels)

    def out(shape, dtype):
        return jax.ShapeDtypeStruct((per_device,) + tuple(shape), dtype)

    work = pltpu.VMEM((3 * batch, count, channels), f32)
    cols = pltpu.VMEM((batch * count, 9 * channels), bf16)
    deltas = pltpu.VMEM((batch * count, channels), bf16)
    grad_shape = (channels, 9 * channels)

    rim_one = jnp.concatenate(
        [features[:, :, 0], features[:, :, -1], features[:, :, :, 0], features[:, :, :, -1]], axis=2
    )
    rim_one = rim_one.transpose(0, 2, 1, 3).reshape(per_device * 4 * pixels, lane_count)
    halo_one = halo_of(rim_one, layout, tile_index).reshape((per_device,) + halo_shape)
    hidden, slope, rim_two = pl.pallas_call(
        first_kernel,
        grid=(per_device,),
        in_specs=[per_tile(tile_shape), per_tile(halo_shape), whole(mat_one.shape), whole((1, channels))],
        out_specs=[per_tile(tile_shape), per_tile(flat_shape), per_tile(rim_shape)],
        out_shape=[out(tile_shape, bf16), out(flat_shape, f32), out(rim_shape, bf16)],
        scratch_shapes=[work],
        compiler_params=pltpu.CompilerParams(**params),
    )(features, halo_one, mat_one, bias_one.reshape(1, channels))
    halo_two = halo_of(rim_two.reshape(-1, lane_count), layout, tile_index)
    output, inner, outer, grad_two, sum_two = pl.pallas_call(
        second_kernel,
        grid=(per_device,),
        in_specs=[
            per_tile(tile_shape), per_tile(halo_shape), per_tile(tile_shape), whole(mat_two.shape),
            whole(flip.shape), whole(sides.shape), whole((1, channels)),
        ],
        out_specs=[
            per_tile(tile_shape), per_tile(flat_shape), per_tile(outer_shape),
            whole(grad_shape), whole((1, channels)),
        ],
        out_shape=[
            out(tile_shape, bf16), out(flat_shape, f32), out(outer_shape, bf16),
            jax.ShapeDtypeStruct(grad_shape, f32), jax.ShapeDtypeStruct((1, channels), f32),
        ],
        scratch_shapes=[work, cols, deltas, pltpu.VMEM((batch, 2, 2 * pixels + 8, channels), f32)],
        compiler_params=pltpu.CompilerParams(**params),
    )(
        hidden, halo_two.reshape((per_device,) + halo_shape), cotangent, mat_two, flip, sides,
        bias_two.reshape(1, channels),
    )
    rim_grad = folded(outer.reshape(-1, lane_count), layout, tile_index, per_device * 4 * pixels)
    grad_one, sum_one = pl.pallas_call(
        third_kernel,
        grid=(per_device,),
        in_specs=[
            per_tile(tile_shape), per_tile(halo_shape), per_tile(flat_shape), per_tile(rim_shape),
            per_tile(flat_shape),
        ],
        out_specs=[whole(grad_shape), whole((1, channels))],
        out_shape=[jax.ShapeDtypeStruct(grad_shape, f32), jax.ShapeDtypeStruct((1, channels), f32)],
        scratch_shapes=[work, cols, deltas],
        compiler_params=pltpu.CompilerParams(**params),
    )(features, halo_one, inner, rim_grad.reshape((per_device,) + rim_shape), slope)

    total_pixels = 12 * S * S * count * batch * samples_count
    grad_scale = 1.0 / math.sqrt(total_pixels)
    devices = device_count * samples_count
    axes = ("tile", "tm")

    def summed(grad, bias):
        rows = jnp.concatenate([grad.reshape(-1, channels), bias], axis=0)
        used = rows.shape[0]
        chunk = -(-used // (8 * devices)) * 8
        rows = jnp.pad(rows, ((0, chunk * devices - used), (0, 0)))
        parts = lax.all_to_all(rows.reshape(devices, chunk, channels), axes, 0, 0)
        mine = (jnp.sum(parts, axis=0) * grad_scale).astype(bf16)
        copies = jnp.broadcast_to(mine[None], (devices, chunk, channels))
        total = lax.all_to_all(copies, axes, 0, 0).reshape(devices * chunk, channels).astype(f32)
        weight = total[: used - 1].reshape(channels, 3, 3, channels).transpose(1, 2, 3, 0)
        return weight, total[used - 1]

    grad_weight_two, grad_bias_two = summed(grad_two, sum_two)
    grad_weight_one, grad_bias_one = summed(grad_one, sum_one)
    return (output, grad_weight_one, grad_bias_one, grad_weight_two, grad_bias_two)


def solution(mesh):
    return jax.shard_map(
        body,
        mesh=mesh,
        in_specs=(
            P("tile", "tm", None, None, None),
            P(),
            P(),
            P(),
            P(),
            P("tile", "tm", None, None, None),
        ),
        out_specs=(P("tile", "tm", None, None, None), P(), P(), P(), P()),
        check_vma=False,
    )
```

profile of v0, /device:TPU:0, one launch (start us, length us, event | category | flops | bytes accessed | tf_op | source)
XLA Modules:
  0.0 216.4 jit_solution(4522354504640045378)
XLA Ops:
  0.6 2.7 %fusion.14 = (bf16[12,4,16,1,128]{4,3,2,1,0:T(2,128)(2,1)S(1)}, bf16[12,4,16,1,128]{4,3,2,1,0:T(2,128)(2,1)S(1)}) fusion(bf16[12,4,16,16,128]{4,3,2,1,0:T(8,128)(2,1)} %x_ref.3), kind=kLoop, calls=%fused_computation.67 | loop fusion | bytes 786432 | tf_op jit(solution)/shard_map/slice | solution.py:423
  6.8 5.1 %collective-permute-start = (bf16[32,512]{1,0:T(8,128)(2,1)S(1)}, bf16[32,512]{1,0:T(8,128)(2,1)S(1)}, u32[]{:S(2)}, u32[]{:S(2)}) collective-permute-start(bf16[32,512]{1,0:T(8,128)(2,1)S(1)} %get-tuple-element.55), channel_id=1, source_target_pairs={{0,24},{2,26},{4,28},{6,30},{8,0},{10,2},{12,4},{14,6},{16,8},{18,... | collective-permute-start | bytes 98312 | tf_op jit(solution)/shard_map/ppermute | solution.py:21
  11.9 1.4 collective-permute-start.2
  19.2 2.5 %collective-permute-start.6 = (bf16[32,512]{1,0:T(8,128)(2,1)S(1)}, bf16[32,512]{1,0:T(8,128)(2,1)S(1)}, u32[]{:S(2)}, u32[]{:S(2)}) collective-permute-start(bf16[32,512]{1,0:T(8,128)(2,1)S(1)} %get-tuple-element.51), channel_id=1, source_target_pairs={{0,6},{2,8},{4,10},{6,12},{8,14},{10,16},{12,18},{14,20},{16,22},{... | collective-permute-start | bytes 98312 | tf_op jit(solution)/shard_map/ppermute | solution.py:21
  24.2 1.6 collective-permute-start.8
  29.7 4.2 %fusion.1 = bf16[1536,512]{1,0:T(8,128)(2,1)S(1)} fusion(bf16[1424,512]{1,0:T(8,128)(2,1)} %constant_dynamic-update-slice_fusion, s32[1536]{0:T(1024)S(1)} %dynamic-slice_reduce_fusion.1), kind=kOutput, calls=%fused_computation.2 | convolution fusion | flops 2241945600 | bytes 3037184 | tf_op jit(solution)/shard_map/dot_general | solution.py:222
  33.9 14.0 %shard_map.155 = (bf16[12,4,16,16,128]{4,3,2,1,0:T(8,128)(2,1)S(1)}, f32[12,4,256,128]{3,2,1,0:T(8,128)}, bf16[12,64,512]{2,1,0:T(8,128)(2,1)S(1)}) custom-call(bf16[12,4,16,16,128]{4,3,2,1,0:T(8,128)(2,1)} %x_ref.3, bf16[12,128,512]{2,1,0:T(8,128)(2,1)S(1)} %bitcast.52, bf16[1152,128]{1,0:T(8,128)(2,1)S(1)} %bitcast.64, f32[1,128]{1,0:T(1,128)S(1)} %bitcast.66), custom_call_target="tpu_custom_call" | custom-call | tf_op jit(solution)/shard_map/pallas_call | solution.py:427
  49.5 2.5 %collective-permute-start.9 = (bf16[32,512]{1,0:T(8,128)(2,1)S(1)}, bf16[32,512]{1,0:T(8,128)(2,1)S(1)}, u32[]{:S(2)}, u32[]{:S(2)}) collective-permute-start(bf16[32,512]{1,0:T(8,128)(2,1)S(1)} %get-tuple-element.47), channel_id=1, source_target_pairs={{0,24},{2,26},{4,28},{6,30},{8,0},{10,2},{12,4},{14,6},{16,8},{18,... | collective-permute-start | bytes 98312 | tf_op jit(solution)/shard_map/ppermute | solution.py:21
  52.1 2.3 %collective-permute-start.11 = (bf16[32,512]{1,0:T(8,128)(2,1)S(1)}, bf16[32,512]{1,0:T(8,128)(2,1)S(1)}, u32[]{:S(2)}, u32[]{:S(2)}) collective-permute-start(bf16[32,512]{1,0:T(8,128)(2,1)S(1)} %get-tuple-element.45), channel_id=1, source_target_pairs={{0,28},{2,30},{4,0},{6,2},{8,4},{10,6},{12,8},{14,10},{16,12},{18,... | collective-permute-start | bytes 98312 | tf_op jit(solution)/shard_map/ppermute | solution.py:21
  54.4 2.5 %collective-permute-start.12 = (bf16[224,512]{1,0:T(8,128)(2,1)S(1)}, bf16[224,512]{1,0:T(8,128)(2,1)S(1)}, u32[]{:S(2)}, u32[]{:S(2)}) collective-permute-start(bf16[224,512]{1,0:T(8,128)(2,1)S(1)} %get-tuple-element.49), channel_id=1, source_target_pairs={{0,30},{2,0},{4,2},{6,4},{8,6},{10,8},{12,10},{14,12},{16,14},{18,... | collective-permute-start | bytes 688136 | tf_op jit(solution)/shard_map/ppermute | solution.py:21
  57.0 1.7 collective-permute-start.15
  58.7 1.5 collective-permute-start.16
  61.1 1.6 collective-permute-start.17
  62.6 3.2 %collective-permute-done.13 = bf16[224,512]{1,0:T(8,128)(2,1)S(1)} collective-permute-done((bf16[224,512]{1,0:T(8,128)(2,1)S(1)}, bf16[224,512]{1,0:T(8,128)(2,1)S(1)}, u32[]{:S(2)}, u32[]{:S(2)}) %collective-permute-start.13) | collective-permute-done | bytes 229408 | tf_op jit(solution)/shard_map/ppermute | solution.py:21
  66.0 2.8 %fusion = bf16[1536,512]{1,0:T(8,128)(2,1)S(1)} fusion(bf16[1424,512]{1,0:T(8,128)(2,1)S(1)} %constant_dynamic-update-slice_fusion.9, s32[1536]{0:T(1024)S(1)} %dynamic-slice_reduce_fusion.1), kind=kOutput, calls=%fused_computation.1 | convolution fusion | flops 2241945600 | bytes 3037184 | tf_op jit(solution)/shard_map/dot_general | solution.py:222
  68.8 34.6 %shard_map.156 = (bf16[12,4,16,16,128]{4,3,2,1,0:T(8,128)(2,1)}, f32[12,4,256,128]{3,2,1,0:T(8,128)}, bf16[12,96,512]{2,1,0:T(8,128)(2,1)S(1)}, f32[128,1152]{1,0:T(8,128)S(1)}, f32[1,128]{1,0:T(1,128)S(1)}) custom-call(bf16[12,4,16,16,128]{4,3,2,1,0:T(8,128)(2,1)} %copy-done, bf16[12,128,512]{2,1,0:T(8,128)(2,1)S(1)} %bitcast.58, ...), custom_call_target="tpu_custom_call" | custom-call | tf_op jit(solution)/shard_map/pallas_call | solution.py:437
  108.4 6.9 %all-to-all-start.2 = ((f32[32,40,128]{2,1,0:T(8,128)}), f32[32,40,128]{2,1,0:T(8,128)S(1)}, u32[]{:S(2)}, u32[]{:S(2)}) async-start(f32[32,40,128]{2,1,0:T(8,128)} %bitcast.23), calls=%async_computation.2 | async-start | bytes 1310720 | tf_op jit(solution)/shard_map/all_to_all | solution.py:482
  115.3 1.6 collective-permute-start.19
  116.9 1.5 collective-permute-start.20
  118.4 4.4 %collective-permute-start.22 = (bf16[224,512]{1,0:T(8,128)(2,1)S(1)}, bf16[224,512]{1,0:T(8,128)(2,1)S(1)}, u32[]{:S(2)}, u32[]{:S(2)}) collective-permute-start(bf16[224,512]{1,0:T(8,128)(2,1)S(1)} %get-tuple-element.40), channel_id=1, source_target_pairs={{0,30},{2,0},{4,2},{6,4},{8,6},{10,8},{12,10},{14,12},{16,14},{18,... | collective-permute-start | bytes 688136 | tf_op jit(solution)/shard_map/ppermute | solution.py:21
  124.0 6.8 %collective-permute-done.19 = bf16[32,512]{1,0:T(8,128)(2,1)S(1)} collective-permute-done((bf16[32,512]{1,0:T(8,128)(2,1)S(1)}, bf16[32,512]{1,0:T(8,128)(2,1)S(1)}, u32[]{:S(2)}, u32[]{:S(2)}) %collective-permute-start.19) | collective-permute-done | bytes 32800 | tf_op jit(solution)/shard_map/ppermute | solution.py:21
  131.4 2.0 collective-permute-done.20
  133.4 3.8 %collective-permute-start.25 = (bf16[32,512]{1,0:T(8,128)(2,1)S(1)}, bf16[32,512]{1,0:T(8,128)(2,1)S(1)}, u32[]{:S(2)}, u32[]{:S(2)}) collective-permute-start(bf16[32,512]{1,0:T(8,128)(2,1)S(1)} %get-tuple-element.34), channel_id=1, source_target_pairs={{0,24},{2,26},{4,28},{6,30},{8,0},{10,2},{12,4},{14,6},{16,8},{18,... | collective-permute-start | bytes 98312 | tf_op jit(solution)/shard_map/ppermute | solution.py:21
  137.8 1.7 collective-permute-start.26
  143.3 3.7 %fusion.2 = f32[768,512]{1,0:T(8,128)S(1)} fusion(bf16[1808,512]{1,0:T(8,128)(2,1)} %constant_dynamic-update-slice_fusion.19, s32[1808]{0:T(1024)S(1)} %dynamic-slice_reduce_fusion), kind=kOutput, calls=%fused_computation.4 | convolution fusion | flops 1423257600 | bytes 3431488 | tf_op jit(solution)/shard_map/dot_general | solution.py:230
  147.0 13.5 %shard_map.157 = (f32[128,1152]{1,0:T(8,128)S(1)}, f32[1,128]{1,0:T(1,128)S(1)}) custom-call(bf16[12,4,16,16,128]{4,3,2,1,0:T(8,128)(2,1)} %x_ref.3, bf16[12,128,512]{2,1,0:T(8,128)(2,1)S(1)} %bitcast.53, f32[12,4,256,128]{3,2,1,0:T(8,128)} %get-tuple-element.18.inner_ref, f32[12,64,512]{2,1,0:T(8,128)S(1)} %bitcast.57, ...), custom_call_target="tpu_custom_call" | custom-call | tf_op jit(solution)/shard_map/pallas_call | solution.py:459
  161.5 3.7 %all-to-all-start = ((f32[32,40,128]{2,1,0:T(8,128)}), f32[32,40,128]{2,1,0:T(8,128)S(1)}, u32[]{:S(2)}, u32[]{:S(2)}) async-start(f32[32,40,128]{2,1,0:T(8,128)} %bitcast.18), calls=%async_computation | async-start | bytes 1310720 | tf_op jit(solution)/shard_map/all_to_all | solution.py:482
  165.3 17.7 %all-to-all-done = f32[32,40,128]{2,1,0:T(8,128)S(1)} async-done(((f32[32,40,128]{2,1,0:T(8,128)}), f32[32,40,128]{2,1,0:T(8,128)S(1)}, u32[]{:S(2)}, u32[]{:S(2)}) %all-to-all-start) | async-done | bytes 655392 | tf_op jit(solution)/shard_map/all_to_all | solution.py:482
  183.8 3.6 %all-to-all-start.3 = ((bf16[32,40,128]{2,1,0:T(8,128)(2,1)}), bf16[32,40,128]{2,1,0:T(8,128)(2,1)S(1)}, u32[]{:S(2)}, u32[]{:S(2)}) async-start(bf16[32,40,128]{2,1,0:T(8,128)(2,1)} %broadcast_in_dim.5), calls=%async_computation.3 | async-start | bytes 655360 | tf_op jit(solution)/shard_map/all_to_all | solution.py:485
  187.5 11.7 %all-to-all-done.3 = bf16[32,40,128]{2,1,0:T(8,128)(2,1)S(1)} async-done(((bf16[32,40,128]{2,1,0:T(8,128)(2,1)}), bf16[32,40,128]{2,1,0:T(8,128)(2,1)S(1)}, u32[]{:S(2)}, u32[]{:S(2)}) %all-to-all-start.3) | async-done | bytes 327712 | tf_op jit(solution)/shard_map/all_to_all | solution.py:485
  199.9 2.7 %all-to-all-start.1 = ((bf16[32,40,128]{2,1,0:T(8,128)(2,1)}), bf16[32,40,128]{2,1,0:T(8,128)(2,1)S(1)}, u32[]{:S(2)}, u32[]{:S(2)}) async-start(bf16[32,40,128]{2,1,0:T(8,128)(2,1)} %broadcast_in_dim.4), calls=%async_computation.1 | async-start | bytes 655360 | tf_op jit(solution)/shard_map/all_to_all | solution.py:485
  204.7 9.7 %all-to-all-done.1 = bf16[32,40,128]{2,1,0:T(8,128)(2,1)S(1)} async-done(((bf16[32,40,128]{2,1,0:T(8,128)(2,1)}), bf16[32,40,128]{2,1,0:T(8,128)(2,1)S(1)}, u32[]{:S(2)}, u32[]{:S(2)}) %all-to-all-start.1) | async-done | bytes 327712 | tf_op jit(solution)/shard_map/all_to_all | solution.py:485
  (123 shorter events, 36.4 us)
Async XLA Ops:
  6.7 9.0 %copy-start.1 = (bf16[3,3,128,128]{3,2,1,0:T(8,128)(2,1)S(1)}, bf16[3,3,128,128]{3,2,1,0:T(8,128)(2,1)}, u32[]{:S(2)}) copy-start(bf16[3,3,128,128]{3,2,1,0:T(8,128)(2,1)} %param.15) | copy-start | bytes 884740
  6.8 11.2 %collective-permute-start = (bf16[32,512]{1,0:T(8,128)(2,1)S(1)}, bf16[32,512]{1,0:T(8,128)(2,1)S(1)}, u32[]{:S(2)}, u32[]{:S(2)}) collective-permute-start(bf16[32,512]{1,0:T(8,128)(2,1)S(1)} %get-tuple-element.55), channel_id=1, source_target_pairs={{0,24},{2,26},{4,28},{6,30},{8,0},{10,2},{12,4},{14,6},{16,8},{18,... | collective-permute-start | bytes 98312 | tf_op jit(solution)/shard_map/ppermute | solution.py:21
  11.9 7.4 %collective-permute-start.1 = (bf16[32,512]{1,0:T(8,128)(2,1)S(1)}, bf16[32,512]{1,0:T(8,128)(2,1)S(1)}, u32[]{:S(2)}, u32[]{:S(2)}) collective-permute-start(bf16[32,512]{1,0:T(8,128)(2,1)S(1)} %get-tuple-element.54), channel_id=1, source_target_pairs={{0,26},{2,28},{4,30},{6,0},{8,2},{10,4},{12,6},{14,8},{16,10},{18,... | collective-permute-start | bytes 98312 | tf_op jit(solution)/shard_map/ppermute | solution.py:21
  11.9 10.5 %collective-permute-start.2 = (bf16[32,512]{1,0:T(8,128)(2,1)S(1)}, bf16[32,512]{1,0:T(8,128)(2,1)S(1)}, u32[]{:S(2)}, u32[]{:S(2)}) collective-permute-start(bf16[32,512]{1,0:T(8,128)(2,1)S(1)} %get-tuple-element.53), channel_id=1, source_target_pairs={{0,28},{2,30},{4,0},{6,2},{8,4},{10,6},{12,8},{14,10},{16,12},{18,... | collective-permute-start | bytes 98312 | tf_op jit(solution)/shard_map/ppermute | solution.py:21
  13.3 10.9 %collective-permute-start.3 = (bf16[224,512]{1,0:T(8,128)(2,1)S(1)}, bf16[224,512]{1,0:T(8,128)(2,1)S(1)}, u32[]{:S(2)}, u32[]{:S(2)}) collective-permute-start(bf16[224,512]{1,0:T(8,128)(2,1)S(1)} %get-tuple-element.57), channel_id=1, source_target_pairs={{0,30},{2,0},{4,2},{6,4},{8,6},{10,8},{12,10},{14,12},{16,14},{18,... | collective-permute-start | bytes 688136 | tf_op jit(solution)/shard_map/ppermute | solution.py:21
  14.7 11.8 %collective-permute-start.4 = (bf16[224,512]{1,0:T(8,128)(2,1)S(1)}, bf16[224,512]{1,0:T(8,128)(2,1)S(1)}, u32[]{:S(2)}, u32[]{:S(2)}) collective-permute-start(bf16[224,512]{1,0:T(8,128)(2,1)S(1)} %get-tuple-element.56), channel_id=1, source_target_pairs={{0,2},{2,4},{4,6},{6,8},{8,10},{10,12},{12,14},{14,16},{16,18},{18... | collective-permute-start | bytes 688136 | tf_op jit(solution)/shard_map/ppermute | solution.py:21
  17.9 9.3 %collective-permute-start.5 = (bf16[32,512]{1,0:T(8,128)(2,1)S(1)}, bf16[32,512]{1,0:T(8,128)(2,1)S(1)}, u32[]{:S(2)}, u32[]{:S(2)}) collective-permute-start(bf16[32,512]{1,0:T(8,128)(2,1)S(1)} %get-tuple-element.52), channel_id=1, source_target_pairs={{0,4},{2,6},{4,8},{6,10},{8,12},{10,14},{12,16},{14,18},{16,20},{1... | collective-permute-start | bytes 98312 | tf_op jit(solution)/shard_map/ppermute | solution.py:21
  19.2 8.6 %collective-permute-start.6 = (bf16[32,512]{1,0:T(8,128)(2,1)S(1)}, bf16[32,512]{1,0:T(8,128)(2,1)S(1)}, u32[]{:S(2)}, u32[]{:S(2)}) collective-permute-start(bf16[32,512]{1,0:T(8,128)(2,1)S(1)} %get-tuple-element.51), channel_id=1, source_target_pairs={{0,6},{2,8},{4,10},{6,12},{8,14},{10,16},{12,18},{14,20},{16,22},{... | collective-permute-start | bytes 98312 | tf_op jit(solution)/shard_map/ppermute | solution.py:21
  22.3 6.1 %collective-permute-start.7 = (bf16[32,512]{1,0:T(8,128)(2,1)S(1)}, bf16[32,512]{1,0:T(8,128)(2,1)S(1)}, u32[]{:S(2)}, u32[]{:S(2)}) collective-permute-start(bf16[32,512]{1,0:T(8,128)(2,1)S(1)} %get-tuple-element.50), channel_id=1, source_target_pairs={{0,8},{2,10},{4,12},{6,14},{8,16},{10,18},{12,20},{14,22},{16,24},... | collective-permute-start | bytes 98312 | tf_op jit(solution)/shard_map/ppermute | solution.py:21
  24.2 4.9 %collective-permute-start.8 = (bf16[16,512]{1,0:T(8,128)(2,1)S(1)}, bf16[16,512]{1,0:T(8,128)(2,1)S(1)}, u32[]{:S(2)}, u32[]{:S(2)}) collective-permute-start(bf16[16,512]{1,0:T(8,128)(2,1)S(1)} %slice.156), channel_id=1, source_target_pairs={{0,16},{2,18},{4,20},{6,22},{8,24},{10,26},{12,28},{14,30},{16,0},... | collective-permute-start | bytes 49160 | tf_op jit(solution)/shard_map/ppermute | solution.py:21
  49.5 7.4 %collective-permute-start.9 = (bf16[32,512]{1,0:T(8,128)(2,1)S(1)}, bf16[32,512]{1,0:T(8,128)(2,1)S(1)}, u32[]{:S(2)}, u32[]{:S(2)}) collective-permute-start(bf16[32,512]{1,0:T(8,128)(2,1)S(1)} %get-tuple-element.47), channel_id=1, source_target_pairs={{0,24},{2,26},{4,28},{6,30},{8,0},{10,2},{12,4},{14,6},{16,8},{18,... | collective-permute-start | bytes 98312 | tf_op jit(solution)/shard_map/ppermute | solution.py:21
  52.1 4.9 %collective-permute-start.10 = (bf16[32,512]{1,0:T(8,128)(2,1)S(1)}, bf16[32,512]{1,0:T(8,128)(2,1)S(1)}, u32[]{:S(2)}, u32[]{:S(2)}) collective-permute-start(bf16[32,512]{1,0:T(8,128)(2,1)S(1)} %get-tuple-element.46), channel_id=1, source_target_pairs={{0,26},{2,28},{4,30},{6,0},{8,2},{10,4},{12,6},{14,8},{16,10},{18,... | collective-permute-start | bytes 98312 | tf_op jit(solution)/shard_map/ppermute | solution.py:21
  52.1 6.5 %collective-permute-start.11 = (bf16[32,512]{1,0:T(8,128)(2,1)S(1)}, bf16[32,512]{1,0:T(8,128)(2,1)S(1)}, u32[]{:S(2)}, u32[]{:S(2)}) collective-permute-start(bf16[32,512]{1,0:T(8,128)(2,1)S(1)} %get-tuple-element.45), channel_id=1, source_target_pairs={{0,28},{2,30},{4,0},{6,2},{8,4},{10,6},{12,8},{14,10},{16,12},{18,... | collective-permute-start | bytes 98312 | tf_op jit(solution)/shard_map/ppermute | solution.py:21
  54.4 6.7 %collective-permute-start.12 = (bf16[224,512]{1,0:T(8,128)(2,1)S(1)}, bf16[224,512]{1,0:T(8,128)(2,1)S(1)}, u32[]{:S(2)}, u32[]{:S(2)}) collective-permute-start(bf16[224,512]{1,0:T(8,128)(2,1)S(1)} %get-tuple-element.49), channel_id=1, source_target_pairs={{0,30},{2,0},{4,2},{6,4},{8,6},{10,8},{12,10},{14,12},{16,14},{18,... | collective-permute-start | bytes 688136 | tf_op jit(solution)/shard_map/ppermute | solution.py:21
  56.9 8.9 %collective-permute-start.13 = (bf16[224,512]{1,0:T(8,128)(2,1)S(1)}, bf16[224,512]{1,0:T(8,128)(2,1)S(1)}, u32[]{:S(2)}, u32[]{:S(2)}) collective-permute-start(bf16[224,512]{1,0:T(8,128)(2,1)S(1)} %get-tuple-element.48), channel_id=1, source_target_pairs={{0,2},{2,4},{4,6},{6,8},{8,10},{10,12},{12,14},{14,16},{16,18},{18... | collective-permute-start | bytes 688136 | tf_op jit(solution)/shard_map/ppermute | solution.py:21
  56.9 8.9 %collective-permute-start.14 = (bf16[32,512]{1,0:T(8,128)(2,1)S(1)}, bf16[32,512]{1,0:T(8,128)(2,1)S(1)}, u32[]{:S(2)}, u32[]{:S(2)}) collective-permute-start(bf16[32,512]{1,0:T(8,128)(2,1)S(1)} %get-tuple-element.44), channel_id=1, source_target_pairs={{0,4},{2,6},{4,8},{6,10},{8,12},{10,14},{12,16},{14,18},{16,20},{1... | collective-permute-start | bytes 98312 | tf_op jit(solution)/shard_map/ppermute | solution.py:21
  57.0 8.9 %collective-permute-start.15 = (bf16[32,512]{1,0:T(8,128)(2,1)S(1)}, bf16[32,512]{1,0:T(8,128)(2,1)S(1)}, u32[]{:S(2)}, u32[]{:S(2)}) collective-permute-start(bf16[32,512]{1,0:T(8,128)(2,1)S(1)} %get-tuple-element.43), channel_id=1, source_target_pairs={{0,6},{2,8},{4,10},{6,12},{8,14},{10,16},{12,18},{14,20},{16,22},{... | collective-permute-start | bytes 98312 | tf_op jit(solution)/shard_map/ppermute | solution.py:21
  58.7 7.2 %collective-permute-start.16 = (bf16[32,512]{1,0:T(8,128)(2,1)S(1)}, bf16[32,512]{1,0:T(8,128)(2,1)S(1)}, u32[]{:S(2)}, u32[]{:S(2)}) collective-permute-start(bf16[32,512]{1,0:T(8,128)(2,1)S(1)} %get-tuple-element.42), channel_id=1, source_target_pairs={{0,8},{2,10},{4,12},{6,14},{8,16},{10,18},{12,20},{14,22},{16,24},... | collective-permute-start | bytes 98312 | tf_op jit(solution)/shard_map/ppermute | solution.py:21
  61.1 4.9 %collective-permute-start.17 = (bf16[16,512]{1,0:T(8,128)(2,1)S(1)}, bf16[16,512]{1,0:T(8,128)(2,1)S(1)}, u32[]{:S(2)}, u32[]{:S(2)}) collective-permute-start(bf16[16,512]{1,0:T(8,128)(2,1)S(1)} %slice.165), channel_id=1, source_target_pairs={{0,16},{2,18},{4,20},{6,22},{8,24},{10,26},{12,28},{14,30},{16,0},... | collective-permute-start | bytes 49160 | tf_op jit(solution)/shard_map/ppermute | solution.py:21
  107.4 15.4 %collective-permute-start.18 = (bf16[32,512]{1,0:T(8,128)(2,1)S(1)}, bf16[32,512]{1,0:T(8,128)(2,1)S(1)}, u32[]{:S(2)}, u32[]{:S(2)}) collective-permute-start(bf16[32,512]{1,0:T(8,128)(2,1)S(1)} %get-tuple-element.39), channel_id=1, source_target_pairs={{0,8},{2,10},{4,12},{6,14},{8,16},{10,18},{12,20},{14,22},{16,24},... | collective-permute-start | bytes 98312 | tf_op jit(solution)/shard_map/ppermute | solution.py:21
  108.4 53.1 %all-to-all-start.2 = ((f32[32,40,128]{2,1,0:T(8,128)}), f32[32,40,128]{2,1,0:T(8,128)S(1)}, u32[]{:S(2)}, u32[]{:S(2)}) async-start(f32[32,40,128]{2,1,0:T(8,128)} %bitcast.23), calls=%async_computation.2 | async-start | bytes 1310720 | tf_op jit(solution)/shard_map/all_to_all | solution.py:482
  115.3 15.5 %collective-permute-start.19 = (bf16[32,512]{1,0:T(8,128)(2,1)S(1)}, bf16[32,512]{1,0:T(8,128)(2,1)S(1)}, u32[]{:S(2)}, u32[]{:S(2)}) collective-permute-start(bf16[32,512]{1,0:T(8,128)(2,1)S(1)} %get-tuple-element.38), channel_id=1, source_target_pairs={{0,6},{2,8},{4,10},{6,12},{8,14},{10,16},{12,18},{14,20},{16,22},{... | collective-permute-start | bytes 98312 | tf_op jit(solution)/shard_map/ppermute | solution.py:21
  116.9 16.5 %collective-permute-start.20 = (bf16[32,512]{1,0:T(8,128)(2,1)S(1)}, bf16[32,512]{1,0:T(8,128)(2,1)S(1)}, u32[]{:S(2)}, u32[]{:S(2)}) collective-permute-start(bf16[32,512]{1,0:T(8,128)(2,1)S(1)} %get-tuple-element.37), channel_id=1, source_target_pairs={{0,4},{2,6},{4,8},{6,10},{8,12},{10,14},{12,16},{14,18},{16,20},{1... | collective-permute-start | bytes 98312 | tf_op jit(solution)/shard_map/ppermute | solution.py:21
  118.4 19.4 %collective-permute-start.21 = (bf16[224,512]{1,0:T(8,128)(2,1)S(1)}, bf16[224,512]{1,0:T(8,128)(2,1)S(1)}, u32[]{:S(2)}, u32[]{:S(2)}) collective-permute-start(bf16[224,512]{1,0:T(8,128)(2,1)S(1)} %get-tuple-element.41), channel_id=1, source_target_pairs={{0,2},{2,4},{4,6},{6,8},{8,10},{10,12},{12,14},{14,16},{16,18},{18... | collective-permute-start | bytes 688136 | tf_op jit(solution)/shard_map/ppermute | solution.py:21
  118.4 21.8 %collective-permute-start.22 = (bf16[224,512]{1,0:T(8,128)(2,1)S(1)}, bf16[224,512]{1,0:T(8,128)(2,1)S(1)}, u32[]{:S(2)}, u32[]{:S(2)}) collective-permute-start(bf16[224,512]{1,0:T(8,128)(2,1)S(1)} %get-tuple-element.40), channel_id=1, source_target_pairs={{0,30},{2,0},{4,2},{6,4},{8,6},{10,8},{12,10},{14,12},{16,14},{18,... | collective-permute-start | bytes 688136 | tf_op jit(solution)/shard_map/ppermute | solution.py:21
  122.8 18.1 %collective-permute-start.23 = (bf16[32,512]{1,0:T(8,128)(2,1)S(1)}, bf16[32,512]{1,0:T(8,128)(2,1)S(1)}, u32[]{:S(2)}, u32[]{:S(2)}) collective-permute-start(bf16[32,512]{1,0:T(8,128)(2,1)S(1)} %get-tuple-element.36), channel_id=1, source_target_pairs={{0,28},{2,30},{4,0},{6,2},{8,4},{10,6},{12,8},{14,10},{16,12},{18,... | collective-permute-start | bytes 98312 | tf_op jit(solution)/shard_map/ppermute | solution.py:21
  130.8 10.7 %collective-permute-start.24 = (bf16[32,512]{1,0:T(8,128)(2,1)S(1)}, bf16[32,512]{1,0:T(8,128)(2,1)S(1)}, u32[]{:S(2)}, u32[]{:S(2)}) collective-permute-start(bf16[32,512]{1,0:T(8,128)(2,1)S(1)} %get-tuple-element.35), channel_id=1, source_target_pairs={{0,26},{2,28},{4,30},{6,0},{8,2},{10,4},{12,6},{14,8},{16,10},{18,... | collective-permute-start | bytes 98312 | tf_op jit(solution)/shard_map/ppermute | solution.py:21
  133.4 8.8 %collective-permute-start.25 = (bf16[32,512]{1,0:T(8,128)(2,1)S(1)}, bf16[32,512]{1,0:T(8,128)(2,1)S(1)}, u32[]{:S(2)}, u32[]{:S(2)}) collective-permute-start(bf16[32,512]{1,0:T(8,128)(2,1)S(1)} %get-tuple-element.34), channel_id=1, source_target_pairs={{0,24},{2,26},{4,28},{6,30},{8,0},{10,2},{12,4},{14,6},{16,8},{18,... | collective-permute-start | bytes 98312 | tf_op jit(solution)/shard_map/ppermute | solution.py:21
  137.8 5.0 %collective-permute-start.26 = (bf16[16,512]{1,0:T(8,128)(2,1)S(1)}, bf16[16,512]{1,0:T(8,128)(2,1)S(1)}, u32[]{:S(2)}, u32[]{:S(2)}) collective-permute-start(bf16[16,512]{1,0:T(8,128)(2,1)S(1)} %slice.176), channel_id=1, source_target_pairs={{0,16},{2,18},{4,20},{6,22},{8,24},{10,26},{12,28},{14,30},{16,0},... | collective-permute-start | bytes 49160 | tf_op jit(solution)/shard_map/ppermute | solution.py:21
  161.5 21.6 %all-to-all-start = ((f32[32,40,128]{2,1,0:T(8,128)}), f32[32,40,128]{2,1,0:T(8,128)S(1)}, u32[]{:S(2)}, u32[]{:S(2)}) async-start(f32[32,40,128]{2,1,0:T(8,128)} %bitcast.18), calls=%async_computation | async-start | bytes 1310720 | tf_op jit(solution)/shard_map/all_to_all | solution.py:482
  183.8 15.3 %all-to-all-start.3 = ((bf16[32,40,128]{2,1,0:T(8,128)(2,1)}), bf16[32,40,128]{2,1,0:T(8,128)(2,1)S(1)}, u32[]{:S(2)}, u32[]{:S(2)}) async-start(bf16[32,40,128]{2,1,0:T(8,128)(2,1)} %broadcast_in_dim.5), calls=%async_computation.3 | async-start | bytes 655360 | tf_op jit(solution)/shard_map/all_to_all | solution.py:485
  199.9 14.4 %all-to-all-start.1 = ((bf16[32,40,128]{2,1,0:T(8,128)(2,1)}), bf16[32,40,128]{2,1,0:T(8,128)(2,1)S(1)}, u32[]{:S(2)}, u32[]{:S(2)}) async-start(bf16[32,40,128]{2,1,0:T(8,128)(2,1)} %broadcast_in_dim.4), calls=%async_computation.1 | async-start | bytes 655360 | tf_op jit(solution)/shard_map/all_to_all | solution.py:485
  (5 other events, 13.6 us)
where the time goes:
time: 218 us; the launch traced here: 216 us
  Pallas kernels  62.1 us (28%)
  starting transfers between devices  56.5 us (26%)
  waiting for transfers between devices  52 us (24%)
  local copies, waits for them, and re-layouts  29.3 us (13%)
  matrix products  13.2 us (6%)
    ppermute x27, starting transfers between devices, passed_along(): return lax.ppermute(value, axis, pairs)  39.6 us
    pallas_call x1, Pallas kernels, body(): pl.pallas_call(second_kernel, grid=(per_device,), in_specs=[per_tile(tile...  34.6 us
    all_to_all x2, waiting for transfers between devices, summed(): lax.all_to_all(copies, axes, 0, 0).reshape(devices * chunk, channels)  21.4 us
    all_to_all x2, waiting for transfers between devices, summed(): parts = lax.all_to_all(rows.reshape(devices, chunk, channels), axes, 0, 0)  17.7 us
    unnamed x41, local copies, waits for them, and re-layouts  16.3 us
    pallas_call x1, Pallas kernels, body(): pl.pallas_call(first_kernel, grid=(per_device,), in_specs=[per_tile(tile_...  14 us
    pallas_call x1, Pallas kernels, body(): pl.pallas_call(third_kernel, grid=(per_device,), in_specs=[per_tile(tile_...  13.5 us
    ppermute x27, waiting for transfers between devices, passed_along(): return lax.ppermute(value, axis, pairs)  12.9 us
  transfers between devices with their start and end apart: 31, of which 7 were waited for; matrix products, arithmetic and copies ran while one was open for 10% of the time, Pallas kernels for 6%

commit v1 on v0

--- a/solution.py
+++ b/solution.py
@@ -1,3 +1,4 @@
+import functools
 import math
 
 import jax
@@ -13,6 +14,8 @@
 
 inv_sqrt_two = 0.7071067811865476
 inv_sqrt_tau = 0.3989422804014327
+LOG2_E = 1.4426950408889634
+MESH = pl.DeviceIdType.MESH
 
 
 def passed_along(value, axis, steps):
@@ -491,18 +494,675 @@
     return (output, grad_weight_one, grad_bias_one, grad_weight_two, grad_bias_two)
 
 
+def cdf_parts(value):
+    bell = jnp.exp2(value * value * (-0.5 * LOG2_E))
+    t = 1.0 / (1.0 + (0.3275911 * inv_sqrt_two) * jnp.abs(value))
+    poly = 0.5 * 1.061405429
+    for coefficient in (-1.453152027, 1.421413741, -0.284496736, 0.254829592):
+        poly = poly * t + 0.5 * coefficient
+    tail = poly * t * bell
+    return jnp.where(value < 0.0, tail, 1.0 - tail), bell
+
+
+def put_shifted(ref, sample, base, rows, left, right):
+    lanes = rows[0].shape[1]
+    half = lax.broadcasted_iota(jnp.int32, (8, lanes), 0)
+    first, last = half == 0, half == 7
+    zero = jnp.zeros((8, lanes), jnp.float32)
+    for t, row in enumerate(rows):
+        low, high = row[:8], row[8:]
+        group, at = 8 * (t // 8), t % 8
+        if left is None:
+            from_left, from_right = zero, zero
+        else:
+            from_left = turned_by(left[group : group + 8], -at)
+            from_right = turned_by(right[group : group + 8], 7 - at)
+        low_down, high_down = turned_by(low, 1), turned_by(high, 1)
+        shifted = jnp.concatenate(
+            [jnp.where(first, from_left, low_down), jnp.where(first, low_down, high_down)], axis=0
+        )
+        ref[sample, base + t, :, 0:lanes] = shifted.astype(jnp.bfloat16)
+        low_up, high_up = turned_by(low, 7), turned_by(high, 7)
+        shifted = jnp.concatenate(
+            [jnp.where(last, high_up, low_up), jnp.where(last, from_right, high_up)], axis=0
+        )
+        ref[sample, base + t, :, 2 * lanes : 3 * lanes] = shifted.astype(jnp.bfloat16)
+
+
+def turned_by(value, steps):
+    steps = steps % 8
+    return value if steps == 0 else pltpu.roll(value, steps, 0)
+
+
+def edges_of(rows):
+    lanes = rows[0].shape[1]
+    half = lax.broadcasted_iota(jnp.int32, (8, lanes), 0)
+    lefts, rights = [], []
+    for group in range(0, len(rows), 8):
+        left = rows[group][:8]
+        right = turned_by(rows[group][8:], 1)
+        for t in range(1, 8):
+            left = jnp.where(half == t, turned_by(rows[group + t][:8], t), left)
+            right = jnp.where(half == t, turned_by(rows[group + t][8:], t + 1), right)
+        lefts.append(left)
+        rights.append(right)
+    return jnp.concatenate(lefts, axis=0), jnp.concatenate(rights, axis=0)
+
+
+def split_pairs(value, channels):
+    rows = []
+    for p in range(value.shape[0] // 16):
+        for e in range(2):
+            rows.append(value[16 * p : 16 * (p + 1), e * channels : (e + 1) * channels])
+    return rows
+
+
+def pair_window(ref, sample, start, pairs):
+    width = ref.shape[3]
+    v = ref[sample, pl.ds(start, 2 * pairs + 2)].reshape(pairs + 1, 2, 16, width)
+    parts = [v[:pairs, 0], v[:pairs, 1], v[1:, 0], v[1:, 1]]
+    return jnp.concatenate([p.reshape(pairs * 16, width) for p in parts], axis=1)
+
+
+def strip_kernel(
+    tm_count,
+    x_hbm, cot_hbm, w1_ref, b1_ref, w2_ref, b2_ref,
+    out_hbm, gw1_ref, gb1_ref, gw2_ref, gb2_ref,
+    field, xs, hs, ds, d1, slope, ghid, w1p, w2p, wback, wside, acc, bias_acc,
+    edge_f, fold_f, edge_send, halo_recv, outer_send, corner_send, outer_recv,
+    grad_send, grad_recv, plane_recv, plane_send, part_send, part_recv,
+    in_sem, cot_sem, out_sem, send_sem, recv_sem, osend_sem, orecv_sem, gsend_sem, grecv_sem,
+):
+    f32, bf16 = jnp.float32, jnp.bfloat16
+    tiles, batch, pixels, _, C = x_hbm.shape
+    height = tiles * pixels
+    columns = 16
+    me = lax.axis_index("tile")
+    other = lax.axis_index("tm")
+    n, j = me // 4, me % 4
+    peers = 4 * tm_count
+    plane = j * tm_count + other
+
+    def wrap(c):
+        return (c + 2 * columns) % columns
+
+    def dma_in(s):
+        return pltpu.make_async_copy(x_hbm.at[:, s], field.at[:, s], in_sem.at[s])
+
+    def dma_cot(s):
+        return pltpu.make_async_copy(cot_hbm.at[:, s], field.at[:, s], cot_sem.at[s])
+
+    def dma_out(s):
+        return pltpu.make_async_copy(field.at[:, s], out_hbm.at[:, s], out_sem.at[s])
+
+    def remote(src, dst, send, recv, device, side=None):
+        pltpu.make_async_remote_copy(
+            src_ref=src, dst_ref=dst, send_sem=send, recv_sem=recv,
+            device_id=(device, other if side is None else side), device_id_type=MESH,
+        ).start()
+
+    def finish(ref, count, sem):
+        view = ref.at[pl.ds(0, count)]
+        pltpu.make_async_copy(view, view, sem).wait()
+
+    for s in range(batch):
+        dma_in(s).start()
+
+    barrier = pltpu.get_barrier_semaphore()
+    for offset in range(1, columns):
+        pl.semaphore_signal(
+            barrier, inc=1, device_id=(wrap(me + offset), other), device_id_type=MESH
+        )
+    for step in range(1, tm_count):
+        for jj in range(4):
+            pl.semaphore_signal(
+                barrier, inc=1, device_id=(4 * n + jj, (other + step) % tm_count),
+                device_id_type=MESH,
+            )
+    pl.semaphore_wait(barrier, columns - 1 + 4 * (tm_count - 1))
+
+    def send_rim(f, s, field_ref, top, bottom):
+        es, er = edge_send.at[f, s, 0], edge_send.at[f, s, 1]
+        ss, rs = send_sem.at[f, s], recv_sem.at[f, s]
+        land = halo_recv.at[f, s]
+
+        def cut(ref, start, count):
+            return ref.at[pl.ds(start, count)]
+
+        @pl.when(j >= 1)
+        def _():
+            remote(cut(es, 16, height), cut(land, height, height), ss, rs, wrap(me - 1))
+
+        @pl.when(j == 0)
+        def _():
+            remote(cut(es, 80, height - 64), cut(land, height, height - 64), ss, rs, wrap(me - 1))
+
+        @pl.when(j <= 2)
+        def _():
+            remote(cut(er, 0, height), cut(land, 0, height), ss, rs, wrap(me + 1))
+
+        @pl.when(j == 3)
+        def _():
+            remote(cut(er, 0, height - 64), cut(land, 64, height - 64), ss, rs, wrap(me + 1))
+
+        remote(top, cut(land, 16 * j, 16), ss, rs, wrap(4 * n + 4))
+        remote(bottom, cut(land, height + 128 + 16 * j, 16), ss, rs, wrap(4 * n - 1))
+        upper, lower = 2 * height, 2 * height + 48
+
+        @pl.when(j == 0)
+        def _():
+            remote(cut(es, 16, 32), cut(land, upper + 16, 32), ss, rs, wrap(me - 4))
+            for jj in range(1, 4):
+                remote(cut(es, 16 * jj, 48), cut(land, upper, 48), ss, rs, wrap(me - 4 + jj))
+            remote(cut(es, 0, 16), cut(land, upper, 16), ss, rs, wrap(me + 8))
+
+        @pl.when(j == 3)
+        def _():
+            for jj in range(3):
+                remote(
+                    cut(er, 112 + 16 * jj, 48), cut(land, lower, 48), ss, rs, wrap(me + 1 + jj)
+                )
+            remote(cut(er, height - 32, 32), cut(land, lower, 32), ss, rs, wrap(me + 4))
+            remote(cut(er, height, 16), cut(land, lower + 32, 16), ss, rs, wrap(me + 8))
+
+    def put_edges(f, s, k, rows):
+        left, right = edges_of(rows)
+        edge_send[f, s, 0, pl.ds(16 + 16 * k, 16), :] = left.astype(bf16)
+        edge_send[f, s, 1, pl.ds(16 * k, 16), :] = right.astype(bf16)
+
+    def put_corners(f, s):
+        row = edge_send[f, s, 0, 16:32, :].astype(f32)
+        edge_send[f, s, 0, 0:16, :] = jnp.broadcast_to(row[0:1], (16, C)).astype(bf16)
+        row = edge_send[f, s, 1, height - 16 : height, :].astype(f32)
+        edge_send[f, s, 1, height : height + 16, :] = jnp.broadcast_to(row[15:16], (16, C)).astype(
+            bf16
+        )
+
+    def put_halo_rows(f, s, ref):
+        for side in range(2):
+            edge_f[0:48, :] = halo_recv[f, s, pl.ds(2 * height + 48 * side, 48), :].astype(f32)
+            for b in range(3):
+                ref[s, side * (height + 1), :, b * C : (b + 1) * C] = edge_f[
+                    15 + b : 31 + b, :
+                ].astype(bf16)
+
+    def shift_tile(f, s, k, ref, rows):
+        left = halo_recv[f, s, pl.ds(16 * k, 16), :].astype(f32)
+        right = halo_recv[f, s, pl.ds(height + 16 * k, 16), :].astype(f32)
+        put_shifted(ref, s, 1 + 16 * k, rows, left, right)
+
+    def features_out(s, carry):
+        dma_in(s).wait()
+
+        def step(k, carry):
+            rows = [field[k, s, t].astype(f32) for t in range(16)]
+            put_edges(0, s, k, rows)
+            return carry
+
+        lax.fori_loop(0, tiles, step, 0)
+        put_corners(0, s)
+        send_rim(0, s, field, field.at[0, s, 0], field.at[tiles - 1, s, pixels - 1])
+        return carry
+
+    lax.fori_loop(0, batch, features_out, 0)
+
+    one, two = w1_ref[...].reshape(9 * C, C), w2_ref[...].reshape(9 * C, C)
+    zeros = jnp.zeros((3 * C, C), bf16)
+    for packed, flat in ((w1p, one), (w2p, two)):
+        packed[0 : 9 * C, 0:C] = flat
+        packed[9 * C : 12 * C, 0:C] = zeros
+        packed[0 : 3 * C, C : 2 * C] = zeros
+        packed[3 * C : 12 * C, C : 2 * C] = flat
+    for e in range(2):
+        gap = 3 * (1 - e)
+        wback[(9 if e == 0 else 0) * C + 0 : (12 if e == 0 else 3) * C, e * C : (e + 1) * C] = zeros
+    for a in range(3):
+        for b in range(3):
+            block = w2_ref[a, b].astype(f32).T.astype(bf16)
+            for e in range(2):
+                at = ((2 + e - a) * 3 + 2 - b) * C
+                wback[at : at + C, e * C : (e + 1) * C] = block
+            if b != 1:
+                wside[b // 2, a * C : (a + 1) * C, :] = block
+
+    bias_one = jnp.concatenate([b1_ref[...], b1_ref[...]], axis=1)
+    bias_two = jnp.concatenate([b2_ref[...], b2_ref[...]], axis=1)
+    bias_acc[...] = jnp.zeros_like(bias_acc)
+
+    def stage_one(s, carry):
+        finish(halo_recv.at[0, s], 2 * height + 96, recv_sem.at[0, s])
+        put_halo_rows(0, s, xs)
+
+        def build(k, carry):
+            for t in range(16):
+                xs[s, 1 + 16 * k + t, :, C : 2 * C] = field[k, s, t]
+            rows = [field[k, s, t].astype(f32) for t in range(16)]
+            shift_tile(0, s, k, xs, rows)
+            return carry
+
+        lax.fori_loop(0, tiles, build, 0)
+
+        def conv(c, carry):
+            pre = jnp.dot(pair_window(xs, s, 32 * c, 16), w1p[...], preferred_element_type=f32)
+            pre = pre + bias_one
+            half, bell = cdf_parts(pre)
+            hidden = pre * half
+            rows = split_pairs(hidden, C)
+            slopes = split_pairs(half + pre * (bell * inv_sqrt_tau), C)
+            for t in range(32):
+                hs[s, 1 + 32 * c + t, :, C : 2 * C] = rows[t].astype(bf16)
+                slope[s, 32 * c + t] = slopes[t]
+            put_edges(1, s, 2 * c, rows[:16])
+            put_edges(1, s, 2 * c + 1, rows[16:])
+            return carry
+
+        lax.fori_loop(0, tiles // 2, conv, 0)
+        put_corners(1, s)
+        top = hs.at[s, 1, :, pl.ds(C, C)]
+        bottom = hs.at[s, height, :, pl.ds(C, C)]
+        send_rim(1, s, hs, top, bottom)
+        @pl.when((j == 0) | (j == 3))
+        def _():
+            finish(all_rows, 544, send_sem.at[0, s])
+
+        @pl.when((j != 0) & (j != 3))
+        def _():
+            finish(all_rows, 416, send_sem.at[0, s])
+
+        dma_cot(s).start()
+        return carry
+
+    all_rows = grad_recv.at[0]
+    lax.fori_loop(0, batch, stage_one, 0)
+
+    for at in (0, 1, height + 2, height + 3, height + 4, height + 5):
+        ds[0, at] = jnp.zeros((pixels, 3 * C), bf16)
+    for side in range(2):
+        edge_f[48 + 240 * side : 48 + 240 * side + 24, :] = jnp.zeros((24, C), f32)
+        edge_f[48 + 240 * side + 24 + height : 288 + 240 * side, :] = jnp.zeros(
+            (216 - height, C), f32
+        )
+    acc[...] = jnp.zeros_like(acc)
+
+    def send_outer(s):
+        ss, rs = osend_sem.at[s], orecv_sem.at[s]
+        ol, orr = outer_send.at[s, 0], outer_send.at[s, 1]
+        tb, bb = corner_send.at[s, 0], corner_send.at[s, 1]
+        land = outer_recv.at[s]
+        g_top, g_bottom, extra = 2 * height, 2 * height + 16, 2 * height + 32
+
+        def cut(ref, start, count):
+            return ref.at[pl.ds(start, count)]
+
+        @pl.when(j >= 1)
+        def _():
+            remote(cut(ol, 16, height), cut(land, height, height), ss, rs, wrap(me - 1))
+
+        @pl.when(j <= 2)
+        def _():
+            remote(cut(orr, 16, height), cut(land, 0, height), ss, rs, wrap(me + 1))
+
+        @pl.when(j == 0)
+        def _():
+            remote(cut(ol, 80, height - 64), cut(land, height, height - 64), ss, rs, wrap(me - 1))
+            for i in range(4):
+                remote(cut(ol, 16 + 16 * i, 16), cut(land, g_top, 16), ss, rs, wrap(me - 4 + i))
+            remote(cut(tb, 0, 16), cut(land, extra + 192, 16), ss, rs, wrap(me + 8))
+
+        @pl.when(j == 3)
+        def _():
+            remote(cut(orr, 16, height - 64), cut(land, 64, height - 64), ss, rs, wrap(me + 1))
+            for i in range(4):
+                remote(
+                    cut(orr, 144 + 16 * i, 16), cut(land, g_bottom, 16), ss, rs, wrap(me + 1 + i)
+                )
+            remote(cut(bb, 32, 16), cut(land, extra + 192, 16), ss, rs, wrap(me + 8))
+
+        remote(tb, cut(land, extra + 48 * j, 48), ss, rs, wrap(4 * n + 4))
+        remote(bb, cut(land, extra + 48 * j, 48), ss, rs, wrap(4 * n - 1))
+
+    def stage_two(s, carry):
+        finish(halo_recv.at[1, s], 2 * height + 96, recv_sem.at[1, s])
+        put_halo_rows(1, s, hs)
+
+        def build(k, carry):
+            rows = [hs[s, 1 + 16 * k + t, :, C : 2 * C].astype(f32) for t in range(16)]
+            shift_tile(1, s, k, hs, rows)
+            return carry
+
+        lax.fori_loop(0, tiles, build, 0)
+        dma_cot(s).wait()
+
+        def conv(c, carry):
+            pre = jnp.dot(pair_window(hs, s, 32 * c, 16), w2p[...], preferred_element_type=f32)
+            pre = pre + bias_two
+            half, bell = cdf_parts(pre)
+            outs = split_pairs(pre * half, C)
+            slopes = split_pairs(half + pre * (bell * inv_sqrt_tau), C)
+            total = jnp.zeros((pixels, C), f32)
+            for q in range(2):
+                deltas = []
+                for t in range(16):
+                    cot = field[2 * c + q, s, t].astype(f32)
+                    delta = cot * slopes[16 * q + t]
+                    field[2 * c + q, s, t] = outs[16 * q + t].astype(bf16)
+                    ds[0, 2 + 32 * c + 16 * q + t, :, C : 2 * C] = delta.astype(bf16)
+                    total = total + delta
+                    deltas.append(delta)
+                put_shifted(ds, 0, 2 + 32 * c + 16 * q, deltas, None, None)
+                left, right = edges_of(deltas)
+                edge_f[pl.ds(72 + 32 * c + 16 * q, 16), :] = left
+                edge_f[pl.ds(312 + 32 * c + 16 * q, 16), :] = right
+            bias_acc[1] += total
+            return carry
+
+        lax.fori_loop(0, tiles // 2, conv, 0)
+        dma_out(s).start()
+
+        fold_f[0:96, :] = jnp.zeros((96, C), f32)
+        for side in range(2):
+            base = 48 + 240 * side
+            lhs = jnp.concatenate(
+                [edge_f[base + 9 - a : base + 233 - a, :] for a in range(3)], axis=1
+            ).astype(bf16)
+            cells = jnp.dot(lhs, wside[side], preferred_element_type=f32)
+            outer_send[s, side] = cells.astype(bf16)
+            fold_f[15 + 17 * side : 16 + 17 * side, :] = cells[15:16]
+            fold_f[63 + 17 * side : 64 + 17 * side, :] = cells[16 + height : 17 + height]
+
+        def back(c, carry):
+            grad = jnp.dot(pair_window(ds, 0, 28 * c, 14), wback[...], preferred_element_type=f32)
+            rows = split_pairs(grad, C)
+            for t in range(28):
+                ghid[s, 28 * c + t] = rows[t]
+            return carry
+
+        lax.fori_loop(0, 7, back, 0)
+        fold_f[16:32, :] = ghid[s, 0]
+        fold_f[64:80, :] = ghid[s, height + 1]
+        corner_send[s, 0] = fold_f[0:48, :].astype(bf16)
+        corner_send[s, 1] = fold_f[48:96, :].astype(bf16)
+        send_outer(s)
+
+        weight_sum(hs, s, ds, 2)
+        return carry
+
+    def weight_sum(ref, s, delta_ref, first):
+        pairs = height // 2
+        if first == 2:
+            v = delta_ref[0, pl.ds(2, height), :, C : 2 * C]
+        else:
+            v = delta_ref[...]
+        v = v.reshape(pairs, 2, 16, C)
+        lhs = jnp.concatenate([v[:, e].reshape(pairs * 16, C) for e in range(2)], axis=1)
+        for w in range(4):
+            x = ref[s, pl.ds(0, height + 2)].reshape(pairs + 1, 2, 16, 3 * C)
+            rhs = (x[:pairs, w] if w < 2 else x[1:, w - 2]).reshape(pairs * 16, 3 * C)
+            acc[:, w * 3 * C : (w + 1) * 3 * C] += lax.dot_general(
+                lhs, rhs, (((0,), (0,)), ((), ())), preferred_element_type=f32
+            )
+
+    lax.fori_loop(0, batch, stage_two, 0)
+
+    share = 9 * C // peers
+    block = share + 16
+
+    def sum_start(g):
+        for i in range(9):
+            at = i * C
+            value = (acc[0:C, at : at + C] + acc[C : 2 * C, at + 3 * C : at + 4 * C]).T.astype(bf16)
+            for u in range(C // 16):
+                row = at + 16 * u
+                grad_send[g, row // share, row % share : row % share + 16, :] = value[
+                    16 * u : 16 * u + 16
+                ]
+        bias = jnp.broadcast_to(
+            jnp.sum(bias_acc[g], axis=0, keepdims=True), (16, C)
+        ).astype(bf16)
+        for d in range(peers):
+            grad_send[g, d, share:block, :] = bias
+        for step in range(1, peers):
+            to = (plane + step) % peers
+            remote(
+                grad_send.at[g, to], grad_recv.at[g, pl.ds(plane * block, block)],
+                gsend_sem.at[g, 0], grecv_sem.at[g, 0], 4 * n + to // tm_count, to % tm_count,
+            )
+        grad_recv[g, pl.ds(plane * block, block), :] = grad_send[g, plane]
+
+    def sum_plane(g):
+        finish(grad_recv.at[g], (peers - 1) * block, grecv_sem.at[g, 0])
+        total = grad_recv[g, 0:block, :].astype(f32)
+        for d in range(1, peers):
+            total = total + grad_recv[g, d * block : (d + 1) * block, :].astype(f32)
+        plane_send[g] = total.astype(bf16)
+        for step in range(1, 4):
+            remote(
+                plane_send.at[g], plane_recv.at[g, pl.ds(n * block, block)],
+                gsend_sem.at[g, 1], grecv_sem.at[g, 1], wrap(me + 4 * step),
+            )
+        plane_recv[g, pl.ds(n * block, block), :] = total.astype(bf16)
+
+    def sum_copies(g, bias_out):
+        finish(plane_recv.at[g], 3 * block, grecv_sem.at[g, 1])
+        total = plane_recv[g, 0:block, :].astype(f32)
+        for d in range(1, 4):
+            total = total + plane_recv[g, d * block : (d + 1) * block, :].astype(f32)
+        pixel_count = 16 * height * pixels * batch * tm_count
+        total = total * (1.0 / math.sqrt(pixel_count))
+        bias_out[...] = total[share : share + 1]
+        mine = total[0:share].astype(bf16)
+        part_send[g] = mine
+        for step in range(1, peers):
+            to = (plane + step) % peers
+            remote(
+                part_send.at[g], part_recv.at[g, pl.ds(plane * share, share)],
+                gsend_sem.at[g, 2], grecv_sem.at[g, 2], 4 * n + to // tm_count, to % tm_count,
+            )
+        part_recv[g, pl.ds(plane * share, share), :] = mine
+
+    def sum_end(g, weight_out):
+        finish(part_recv.at[g], (peers - 1) * share, grecv_sem.at[g, 2])
+        weight_out[...] = part_recv[g].astype(f32)
+        finish(grad_recv.at[g], (peers - 1) * block, gsend_sem.at[g, 0])
+        finish(plane_recv.at[g], 3 * block, gsend_sem.at[g, 1])
+        finish(part_recv.at[g], (peers - 1) * share, gsend_sem.at[g, 2])
+
+    sum_start(1)
+    acc[...] = jnp.zeros_like(acc)
+
+    def stage_three(s, carry):
+        @pl.when((j == 0) | (j == 3))
+        def _():
+            finish(all_rows, 560, orecv_sem.at[s])
+
+        @pl.when((j != 0) & (j != 3))
+        def _():
+            finish(all_rows, 416, orecv_sem.at[s])
+
+        extra = 2 * height + 32
+        left_at, right_at = 16, 240
+
+        @pl.when(j != 0)
+        def _():
+            fold_f[left_at : left_at + height, :] = outer_recv[s, 0:height, :].astype(f32)
+
+        @pl.when(j == 0)
+        def _():
+            fold_f[left_at - 16 : left_at + 64, :] = jnp.zeros((80, C), f32)
+            fold_f[left_at + 64 : left_at + height, :] = outer_recv[s, 64:height, :].astype(f32)
+            for jj in range(4):
+                at = left_at - 16 + 16 * jj
+                fold_f[at : at + 48, :] += outer_recv[
+                    s, extra + 48 * jj : extra + 48 * jj + 48, :
+                ].astype(f32)
+            corner = outer_recv[s, extra + 192 : extra + 208, :].astype(f32)
+            fold_f[left_at : left_at + 1, :] += corner[15:16]
+
+        @pl.when(j != 3)
+        def _():
+            fold_f[right_at : right_at + height, :] = outer_recv[s, height : 2 * height, :].astype(
+                f32
+            )
+
+        @pl.when(j == 3)
+        def _():
+            fold_f[right_at : right_at + height - 64, :] = outer_recv[
+                s, height : 2 * height - 64, :
+            ].astype(f32)
+            fold_f[right_at + height - 64 : right_at + height + 16, :] = jnp.zeros((80, C), f32)
+            for jj in range(4):
+                at = right_at + 112 + 16 * jj
+                fold_f[at : at + 48, :] += outer_recv[
+                    s, extra + 48 * jj : extra + 48 * jj + 48, :
+                ].astype(f32)
+            corner = outer_recv[s, extra + 192 : extra + 208, :].astype(f32)
+            last = right_at + height - 1
+            fold_f[last : last + 1, :] += corner[0:1]
+
+        ghid[s, 1] += outer_recv[s, 2 * height : 2 * height + 16, :].astype(f32)
+        ghid[s, height] += outer_recv[s, 2 * height + 16 : 2 * height + 32, :].astype(f32)
+
+        def scale(k, carry):
+            total = jnp.zeros((pixels, C), f32)
+            half = lax.broadcasted_iota(jnp.int32, (8, C), 0)
+            for t in range(16):
+                if t % 8 == 0:
+                    left = fold_f[pl.ds(left_at + 16 * k + t, 8), :]
+                    right = fold_f[pl.ds(right_at + 16 * k + t, 8), :]
+                at = t % 8
+                value = ghid[s, 1 + 16 * k + t]
+                low = value[:8] + jnp.where(half == 0, turned_by(left, -at), 0.0)
+                high = value[8:] + jnp.where(half == 7, turned_by(right, 7 - at), 0.0)
+                delta = jnp.concatenate([low, high], axis=0) * slope[s, 16 * k + t]
+                d1[16 * k + t] = delta.astype(bf16)
+                total = total + delta
+            bias_acc[0] += total
+            return carry
+
+        lax.fori_loop(0, tiles, scale, 0)
+        weight_sum(xs, s, d1, 0)
+
+        @pl.when(s == 0)
+        def _():
+            sum_plane(1)
+
+        @pl.when(s == min(1, batch - 1))
+        def _():
+            sum_copies(1, gb2_ref)
+
+        return carry
+
+    lax.fori_loop(0, batch, stage_three, 0)
+    sum_start(0)
+    sum_end(1, gw2_ref)
+
+    for s in range(batch):
+        dma_out(s).wait()
+
+        @pl.when((j == 0) | (j == 3))
+        def _():
+            finish(all_rows, 544, send_sem.at[1, s])
+            finish(all_rows, 496, osend_sem.at[s])
+
+        @pl.when((j != 0) & (j != 3))
+        def _():
+            finish(all_rows, 416, send_sem.at[1, s])
+            finish(all_rows, 480, osend_sem.at[s])
+
+    sum_plane(0)
+    sum_copies(0, gb1_ref)
+    sum_end(0, gw1_ref)
+
+
+def strip_body(features, weight_one, bias_one, weight_two, bias_two, cotangent):
+    tm_count = lax.axis_size("tm")
+    tiles, batch, pixels, _, C = features.shape
+    height = tiles * pixels
+    bf16, f32 = jnp.bfloat16, jnp.float32
+    peers = 4 * tm_count
+    share = 9 * C // peers
+    block = share + 16
+    vmem = pl.BlockSpec(memory_space=pltpu.VMEM)
+    hbm = pl.BlockSpec(memory_space=pl.ANY)
+    dma = pltpu.SemaphoreType.DMA
+    flops = 10 * tiles * batch * pixels * pixels * 9 * C * C
+    output, gw1, gb1, gw2, gb2 = pl.pallas_call(
+        functools.partial(strip_kernel, tm_count),
+        in_specs=[hbm, hbm, vmem, vmem, vmem, vmem],
+        out_specs=[hbm, vmem, vmem, vmem, vmem],
+        out_shape=[
+            jax.ShapeDtypeStruct(features.shape, bf16),
+            jax.ShapeDtypeStruct((9 * C, C), f32), jax.ShapeDtypeStruct((1, C), f32),
+            jax.ShapeDtypeStruct((9 * C, C), f32), jax.ShapeDtypeStruct((1, C), f32),
+        ],
+        scratch_shapes=[
+            pltpu.VMEM(features.shape, bf16),
+            pltpu.VMEM((batch, height + 2, pixels, 3 * C), bf16),
+            pltpu.VMEM((batch, height + 2, pixels, 3 * C), bf16),
+            pltpu.VMEM((1, height + 6, pixels, 3 * C), bf16),
+            pltpu.VMEM((height, pixels, C), bf16),
+            pltpu.VMEM((batch, height, pixels, C), f32),
+            pltpu.VMEM((batch, height + 4, pixels, C), f32),
+            pltpu.VMEM((12 * C, 2 * C), bf16),
+            pltpu.VMEM((12 * C, 2 * C), bf16),
+            pltpu.VMEM((12 * C, 2 * C), bf16),
+            pltpu.VMEM((2, 3 * C, C), bf16),
+            pltpu.VMEM((2 * C, 12 * C), f32),
+            pltpu.VMEM((2, pixels, C), f32),
+            pltpu.VMEM((528, C), f32),
+            pltpu.VMEM((464, C), f32),
+            pltpu.VMEM((2, batch, 2, height + 16, C), bf16),
+            pltpu.VMEM((2, batch, 2 * height + 96, C), bf16),
+            pltpu.VMEM((batch, 2, height + 32, C), bf16),
+            pltpu.VMEM((batch, 2, 48, C), bf16),
+            pltpu.VMEM((batch, 2 * height + 240, C), bf16),
+            pltpu.VMEM((2, peers, block, C), bf16),
+            pltpu.VMEM((2, peers * block, C), bf16),
+            pltpu.VMEM((2, 4 * block, C), bf16),
+            pltpu.VMEM((2, block, C), bf16),
+            pltpu.VMEM((2, share, C), bf16),
+            pltpu.VMEM((2, 9 * C, C), bf16),
+            dma((batch,)), dma((batch,)), dma((batch,)),
+            dma((2, batch)), dma((2, batch)), dma((batch,)), dma((batch,)), dma((2, 3)), dma((2, 3)),
+        ],
+        compiler_params=pltpu.CompilerParams(
+            collective_id=0, has_side_effects=True, vmem_limit_bytes=60 * 1024 * 1024
+        ),
+        cost_estimate=pl.CostEstimate(
+            flops=flops, bytes_accessed=6 * features.size, transcendentals=4 * features.size
+        ),
+    )(
+        features, cotangent, weight_one, bias_one.reshape(1, C), weight_two,
+        bias_two.reshape(1, C),
+    )
+    shape = weight_one.shape
+    return (output, gw1.reshape(shape), gb1.reshape(C), gw2.reshape(shape), gb2.reshape(C))
+
+
+def whole_columns(mesh, tiles):
+    columns, samples = mesh.shape["tile"], mesh.shape["tm"]
+    return columns == 4 * S and tiles == 3 * S * columns and samples in (1, 2)
+
+
 def solution(mesh):
-    return jax.shard_map(
-        body,
-        mesh=mesh,
-        in_specs=(
-            P("tile", "tm", None, None, None),
-            P(),
-            P(),
-            P(),
-            P(),
-            P("tile", "tm", None, None, None),
-        ),
-        out_specs=(P("tile", "tm", None, None, None), P(), P(), P(), P()),
-        check_vma=False,
-    )
+    def call(*arrays):
+        if whole_columns(mesh, arrays[0].shape[0]):
+            chosen = strip_body
+        else:
+            chosen = body
+        return jax.shard_map(
+            chosen,
+            mesh=mesh,
+            in_specs=(
+                P("tile", "tm", None, None, None),
+                P(),
+                P(),
+                P(),
+                P(),
+                P("tile", "tm", None, None, None),
+            ),
+            out_specs=(P("tile", "tm", None, None, None), P(), P(), P(), P()),
+            check_vma=False,
+        )(*arrays)
+
+    return call

time: 218 us -> 103 us (0.47)
  starting transfers between devices: 56.5 us -> 0 us
  waiting for transfers between devices: 52 us -> 0 us
  Pallas kernels: 62.1 us -> 94.9 us
  local copies, waits for them, and re-layouts: 29.3 us -> 7.26 us
  matrix products: 13.2 us -> 0 us
    ppermute x27 -> x0, starting transfers between devices: 39.6 us -> none  [passed_along(): return lax.ppermute(value, axis, pairs)]
    all_to_all x4 -> x0, waiting for transfers between devices: 39.1 us -> none  [the longest x2 21.4 us: summed(): lax.all_to_all(copies, axes, 0, 0).reshape(devices * chunk, channels)]
    pallas_call x3 -> x1, Pallas kernels: 62.1 us -> 94.9 us  [strip_body(): pl.pallas_call(functools.partial(strip_kernel, tm_count), in_specs=[hbm,...]
    all_to_all x4 -> x0, starting transfers between devices: 16.9 us -> none  [the longest x2 10.6 us: summed(): parts = lax.all_to_all(rows.reshape(devices, chunk, channels), axes, 0, 0)]
    dot_general x6 -> x0, matrix products: 13.2 us -> none  [the longest x2 6.96 us: halo_of(): return jnp.dot(one_hot(receive, tile_index, pool.shape[0]), pool)]
    ppermute x27 -> x0, waiting for transfers between devices: 12.9 us -> none  [passed_along(): return lax.ppermute(value, axis, pairs)]
    unnamed x41 -> x13, local copies, waits for them, and re-layouts: 16.3 us -> 7.26 us
    slice x15 -> x0, local copies, waits for them, and re-layouts: 3.17 us -> none  [the longest x1 2.67 us: body(): features[:, :, :, 0]]
  transfers between devices with their start and end apart: 31 -> 0, of which waited for: 7 -> 0; matrix products, arithmetic and copies ran while one was open for 10% -> 0% of each run, Pallas kernels for 6% -> 0%
where the time goes in v1:
time: 103 us
  Pallas kernels  94.9 us (92%)
  local copies, waits for them, and re-layouts  7.26 us (7%)
    pallas_call x1, Pallas kernels, strip_body(): pl.pallas_call(functools.partial(strip_kernel, tm_count), in_specs=[hbm,...  94.9 us
    unnamed x13, local copies, waits for them, and re-layouts  7.26 us

profile of v1, /device:TPU:0, one launch (start us, length us, event | category | flops | bytes accessed | tf_op | source)
XLA Modules:
  0.0 102.9 jit_solution(4786954026288121102)
XLA Ops:
  0.6 94.9 %shard_map.101 = (bf16[12,4,16,16,128]{4,3,2,1,0:T(8,128)(2,1)}, f32[1152,128]{1,0:T(8,128)}, f32[1,128]{1,0:T(1,128)}, f32[1152,128]{1,0:T(8,128)}, f32[1,128]{1,0:T(1,128)}) custom-call(bf16[12,4,16,16,128]{4,3,2,1,0:T(8,128)(2,1)} %x_hbm.1, bf16[12,4,16,16,128]{4,3,2,1,0:T(8,128)(2,1)} %cot_hbm.1, bf16[3,3,128,128]{3,2,1,0:T(8,128)(2,1)} %w1_ref.1, ...), custom_call_target="tpu_custom_call" | custom-call | flops 18119393280 | bytes 9437184 | tf_op jit(solution)/shard_map/pallas_call | solution.py:1089
  95.6 0.0 copy-start.1
  95.6 0.0 copy-start.3
  95.6 0.0 copy-start
  95.6 0.0 copy-start.2
  95.6 4.6 %copy.16 = bf16[12,4,16,16,128]{4,3,2,1,0:T(8,128)(2,1)} copy(bf16[12,4,16,16,128]{4,3,2,1,0:T(8,128)(2,1)} %get-tuple-element.20) | data formatting | bytes 6291456
  100.2 0.0 copy-done.1
  100.2 0.8 copy.17
  101.0 0.0 copy-done.3
  101.0 0.5 copy.18
  101.6 0.0 copy-done
  101.6 0.8 copy.19
  102.4 0.0 copy-done.2
  102.4 0.5 copy.20
Async XLA Ops:
  95.6 4.6 %copy-start.1 = (f32[1152,128]{1,0:T(8,128)S(1)}, f32[1152,128]{1,0:T(8,128)}, u32[]{:S(2)}) copy-start(f32[1152,128]{1,0:T(8,128)} %get-tuple-element.11) | copy-start | bytes 1769476
  95.6 5.4 %copy-start.3 = (f32[1,128]{1,0:T(1,128)S(1)}, f32[1,128]{1,0:T(1,128)}, u32[]{:S(2)}) copy-start(f32[1,128]{1,0:T(1,128)} %get-tuple-element.12) | copy-start | bytes 1540
  95.6 6.0 %copy-start = (f32[1152,128]{1,0:T(8,128)S(1)}, f32[1152,128]{1,0:T(8,128)}, u32[]{:S(2)}) copy-start(f32[1152,128]{1,0:T(8,128)} %get-tuple-element.13) | copy-start | bytes 1769476
  95.6 6.8 %copy-start.2 = (f32[1,128]{1,0:T(1,128)S(1)}, f32[1,128]{1,0:T(1,128)}, u32[]{:S(2)}) copy-start(f32[1,128]{1,0:T(1,128)} %get-tuple-element.14) | copy-start | bytes 1540

commit v2 on v1

--- a/solution.py
+++ b/solution.py
@@ -504,29 +504,18 @@
     return jnp.where(value < 0.0, tail, 1.0 - tail), bell
 
 
-def put_shifted(ref, sample, base, rows, left, right):
-    lanes = rows[0].shape[1]
-    half = lax.broadcasted_iota(jnp.int32, (8, lanes), 0)
-    first, last = half == 0, half == 7
-    zero = jnp.zeros((8, lanes), jnp.float32)
-    for t, row in enumerate(rows):
-        low, high = row[:8], row[8:]
-        group, at = 8 * (t // 8), t % 8
-        if left is None:
-            from_left, from_right = zero, zero
-        else:
-            from_left = turned_by(left[group : group + 8], -at)
-            from_right = turned_by(right[group : group + 8], 7 - at)
-        low_down, high_down = turned_by(low, 1), turned_by(high, 1)
-        shifted = jnp.concatenate(
-            [jnp.where(first, from_left, low_down), jnp.where(first, low_down, high_down)], axis=0
-        )
-        ref[sample, base + t, :, 0:lanes] = shifted.astype(jnp.bfloat16)
-        low_up, high_up = turned_by(low, 7), turned_by(high, 7)
-        shifted = jnp.concatenate(
-            [jnp.where(last, high_up, low_up), jnp.where(last, from_right, high_up)], axis=0
-        )
-        ref[sample, base + t, :, 2 * lanes : 3 * lanes] = shifted.astype(jnp.bfloat16)
+def put_shifted(ref, sample, at, row, first, last, from_left, from_right):
+    low, high = row[:8], row[8:]
+    low_down, high_down = turned_by(low, 1), turned_by(high, 1)
+    shifted = jnp.concatenate(
+        [jnp.where(first, from_left, low_down), jnp.where(first, low_down, high_down)], axis=0
+    )
+    ref[sample, at, 0] = shifted.astype(jnp.bfloat16)
+    low_up, high_up = turned_by(low, 7), turned_by(high, 7)
+    shifted = jnp.concatenate(
+        [jnp.where(last, high_up, low_up), jnp.where(last, from_right, high_up)], axis=0
+    )
+    ref[sample, at, 2] = shifted.astype(jnp.bfloat16)
 
 
 def turned_by(value, steps):
@@ -534,41 +523,37 @@
     return value if steps == 0 else pltpu.roll(value, steps, 0)
 
 
-def edges_of(rows):
-    lanes = rows[0].shape[1]
-    half = lax.broadcasted_iota(jnp.int32, (8, lanes), 0)
-    lefts, rights = [], []
-    for group in range(0, len(rows), 8):
-        left = rows[group][:8]
-        right = turned_by(rows[group][8:], 1)
-        for t in range(1, 8):
-            left = jnp.where(half == t, turned_by(rows[group + t][:8], t), left)
-            right = jnp.where(half == t, turned_by(rows[group + t][8:], t + 1), right)
-        lefts.append(left)
-        rights.append(right)
-    return jnp.concatenate(lefts, axis=0), jnp.concatenate(rights, axis=0)
-
-
-def split_pairs(value, channels):
-    rows = []
-    for p in range(value.shape[0] // 16):
-        for e in range(2):
-            rows.append(value[16 * p : 16 * (p + 1), e * channels : (e + 1) * channels])
-    return rows
+class Edges:
+    def __init__(self, half):
+        self.half, self.lefts, self.rights = half, [], []
+
+    def add(self, t, row):
+        if t % 8 == 0:
+            self.lefts.append(row[:8])
+            self.rights.append(turned_by(row[8:], 1))
+        else:
+            here = self.half == t % 8
+            self.lefts[-1] = jnp.where(here, turned_by(row[:8], t), self.lefts[-1])
+            self.rights[-1] = jnp.where(here, turned_by(row[8:], t + 1), self.rights[-1])
+
+    def columns(self):
+        return jnp.concatenate(self.lefts, axis=0), jnp.concatenate(self.rights, axis=0)
 
 
 def pair_window(ref, sample, start, pairs):
-    width = ref.shape[3]
-    v = ref[sample, pl.ds(start, 2 * pairs + 2)].reshape(pairs + 1, 2, 16, width)
+    lanes = ref.shape[4]
+    v = ref[sample, pl.ds(start, 2 * pairs + 2)].reshape(pairs + 1, 2, 3, 16, lanes)
     parts = [v[:pairs, 0], v[:pairs, 1], v[1:, 0], v[1:, 1]]
-    return jnp.concatenate([p.reshape(pairs * 16, width) for p in parts], axis=1)
+    return jnp.concatenate(
+        [p[:, b].reshape(pairs * 16, lanes) for p in parts for b in range(3)], axis=1
+    )
 
 
 def strip_kernel(
     tm_count,
     x_hbm, cot_hbm, w1_ref, b1_ref, w2_ref, b2_ref,
     out_hbm, gw1_ref, gb1_ref, gw2_ref, gb2_ref,
-    field, xs, hs, ds, d1, slope, ghid, w1p, w2p, wback, wside, acc, bias_acc,
+    field, xs, hs, ds, d1, turned, slope, ghid, pre_f, w1p, w2p, wback, wside, acc, bias_acc,
     edge_f, fold_f, edge_send, halo_recv, outer_send, corner_send, outer_recv,
     grad_send, grad_recv, plane_recv, plane_send, part_send, part_recv,
     in_sem, cot_sem, out_sem, send_sem, recv_sem, osend_sem, orecv_sem, gsend_sem, grecv_sem,
@@ -665,8 +650,11 @@
             remote(cut(er, height - 32, 32), cut(land, lower, 32), ss, rs, wrap(me + 4))
             remote(cut(er, height, 16), cut(land, lower + 32, 16), ss, rs, wrap(me + 8))
 
-    def put_edges(f, s, k, rows):
-        left, right = edges_of(rows)
+    half_iota = lax.broadcasted_iota(jnp.int32, (8, C), 0)
+    first_pixel, last_pixel = half_iota == 0, half_iota == 7
+
+    def put_edges(f, s, k, edges):
+        left, right = edges.columns()
         edge_send[f, s, 0, pl.ds(16 + 16 * k, 16), :] = left.astype(bf16)
         edge_send[f, s, 1, pl.ds(16 * k, 16), :] = right.astype(bf16)
 
@@ -682,21 +670,28 @@
         for side in range(2):
             edge_f[0:48, :] = halo_recv[f, s, pl.ds(2 * height + 48 * side, 48), :].astype(f32)
             for b in range(3):
-                ref[s, side * (height + 1), :, b * C : (b + 1) * C] = edge_f[
+                ref[s, side * (height + 1), b] = edge_f[
                     15 + b : 31 + b, :
                 ].astype(bf16)
 
-    def shift_tile(f, s, k, ref, rows):
+    def shift_tile(f, s, k, ref, row_of):
         left = halo_recv[f, s, pl.ds(16 * k, 16), :].astype(f32)
         right = halo_recv[f, s, pl.ds(height + 16 * k, 16), :].astype(f32)
-        put_shifted(ref, s, 1 + 16 * k, rows, left, right)
+        for t in range(16):
+            group = 8 * (t // 8)
+            put_shifted(
+                ref, s, 1 + 16 * k + t, row_of(t), first_pixel, last_pixel,
+                turned_by(left[group : group + 8], -t), turned_by(right[group : group + 8], 7 - t),
+            )
 
     def features_out(s, carry):
         dma_in(s).wait()
 
         def step(k, carry):
-            rows = [field[k, s, t].astype(f32) for t in range(16)]
-            put_edges(0, s, k, rows)
+            edges = Edges(half_iota)
+            for t in range(16):
+                edges.add(t, field[k, s, t].astype(f32))
+            put_edges(0, s, k, edges)
             return carry
 
         lax.fori_loop(0, tiles, step, 0)
@@ -735,31 +730,38 @@
 
         def build(k, carry):
             for t in range(16):
-                xs[s, 1 + 16 * k + t, :, C : 2 * C] = field[k, s, t]
-            rows = [field[k, s, t].astype(f32) for t in range(16)]
-            shift_tile(0, s, k, xs, rows)
+                xs[s, 1 + 16 * k + t, 1] = field[k, s, t]
+            shift_tile(0, s, k, xs, lambda t: field[k, s, t].astype(f32))
             return carry
 
         lax.fori_loop(0, tiles, build, 0)
 
-        def conv(c, carry):
-            pre = jnp.dot(pair_window(xs, s, 32 * c, 16), w1p[...], preferred_element_type=f32)
-            pre = pre + bias_one
-            half, bell = cdf_parts(pre)
-            hidden = pre * half
-            rows = split_pairs(hidden, C)
-            slopes = split_pairs(half + pre * (bell * inv_sqrt_tau), C)
-            for t in range(32):
-                hs[s, 1 + 32 * c + t, :, C : 2 * C] = rows[t].astype(bf16)
-                slope[s, 32 * c + t] = slopes[t]
-            put_edges(1, s, 2 * c, rows[:16])
-            put_edges(1, s, 2 * c + 1, rows[16:])
-            return carry
-
-        lax.fori_loop(0, tiles // 2, conv, 0)
+        def dot(c):
+            pre_f[rows_of * c : rows_of * (c + 1), :] = jnp.dot(
+                pair_window(xs, s, 2 * per_chunk * c, per_chunk), w1p[...],
+                preferred_element_type=f32,
+            )
+
+        def after(k):
+            edges = Edges(half_iota)
+            for q in range(8):
+                at = 128 * k + 16 * q
+                pre = pre_f[at : at + 16, :] + bias_one
+                half, bell = cdf_parts(pre)
+                hidden = pre * half
+                slopes = half + pre * (bell * inv_sqrt_tau)
+                for e in range(2):
+                    t = 2 * q + e
+                    row = hidden[:, e * C : (e + 1) * C]
+                    hs[s, 1 + 16 * k + t, 1] = row.astype(bf16)
+                    slope[s, 16 * k + t] = slopes[:, e * C : (e + 1) * C]
+                    edges.add(t, row)
+            put_edges(1, s, k, edges)
+
+        in_turn(dot, after)
         put_corners(1, s)
-        top = hs.at[s, 1, :, pl.ds(C, C)]
-        bottom = hs.at[s, height, :, pl.ds(C, C)]
+        top = hs.at[s, 1, 1]
+        bottom = hs.at[s, height, 1]
         send_rim(1, s, hs, top, bottom)
         @pl.when((j == 0) | (j == 3))
         def _():
@@ -772,17 +774,28 @@
         dma_cot(s).start()
         return carry
 
-    all_rows = grad_recv.at[0]
+    all_rows = outer_recv.at[0]
+    chunks = 3
+    per_chunk = height // 2 // chunks
+    rows_of = 16 * per_chunk
+
+    def in_turn(dot, after):
+        for c in range(chunks + 1):
+            if c < chunks:
+                dot(c)
+            if c > 0:
+                for k in range(tiles // chunks * (c - 1), tiles // chunks * c):
+                    after(k)
+
     lax.fori_loop(0, batch, stage_one, 0)
 
-    for at in (0, 1, height + 2, height + 3, height + 4, height + 5):
-        ds[0, at] = jnp.zeros((pixels, 3 * C), bf16)
+    for at in (0, 1, height + 2, height + 3):
+        ds[0, at] = jnp.zeros((3, pixels, C), bf16)
     for side in range(2):
         edge_f[48 + 240 * side : 48 + 240 * side + 24, :] = jnp.zeros((24, C), f32)
         edge_f[48 + 240 * side + 24 + height : 288 + 240 * side, :] = jnp.zeros(
             (216 - height, C), f32
         )
-    acc[...] = jnp.zeros_like(acc)
 
     def send_outer(s):
         ss, rs = osend_sem.at[s], orecv_sem.at[s]
@@ -826,37 +839,44 @@
         put_halo_rows(1, s, hs)
 
         def build(k, carry):
-            rows = [hs[s, 1 + 16 * k + t, :, C : 2 * C].astype(f32) for t in range(16)]
-            shift_tile(1, s, k, hs, rows)
+            shift_tile(1, s, k, hs, lambda t: hs[s, 1 + 16 * k + t, 1].astype(f32))
             return carry
 
         lax.fori_loop(0, tiles, build, 0)
         dma_cot(s).wait()
 
-        def conv(c, carry):
-            pre = jnp.dot(pair_window(hs, s, 32 * c, 16), w2p[...], preferred_element_type=f32)
-            pre = pre + bias_two
-            half, bell = cdf_parts(pre)
-            outs = split_pairs(pre * half, C)
-            slopes = split_pairs(half + pre * (bell * inv_sqrt_tau), C)
+        def dot(c):
+            pre_f[rows_of * c : rows_of * (c + 1), :] = jnp.dot(
+                pair_window(hs, s, 2 * per_chunk * c, per_chunk), w2p[...],
+                preferred_element_type=f32,
+            )
+
+        zero = jnp.zeros((8, C), f32)
+
+        def after(k):
+            edges = Edges(half_iota)
             total = jnp.zeros((pixels, C), f32)
-            for q in range(2):
-                deltas = []
-                for t in range(16):
-                    cot = field[2 * c + q, s, t].astype(f32)
-                    delta = cot * slopes[16 * q + t]
-                    field[2 * c + q, s, t] = outs[16 * q + t].astype(bf16)
-                    ds[0, 2 + 32 * c + 16 * q + t, :, C : 2 * C] = delta.astype(bf16)
+            for q in range(8):
+                at = 128 * k + 16 * q
+                pre = pre_f[at : at + 16, :] + bias_two
+                half, bell = cdf_parts(pre)
+                outs = pre * half
+                slopes = half + pre * (bell * inv_sqrt_tau)
+                for e in range(2):
+                    t = 2 * q + e
+                    delta = field[k, s, t].astype(f32) * slopes[:, e * C : (e + 1) * C]
+                    field[k, s, t] = outs[:, e * C : (e + 1) * C].astype(bf16)
+                    row = 2 + 16 * k + t
+                    ds[0, row, 1] = delta.astype(bf16)
                     total = total + delta
-                    deltas.append(delta)
-                put_shifted(ds, 0, 2 + 32 * c + 16 * q, deltas, None, None)
-                left, right = edges_of(deltas)
-                edge_f[pl.ds(72 + 32 * c + 16 * q, 16), :] = left
-                edge_f[pl.ds(312 + 32 * c + 16 * q, 16), :] = right
+                    put_shifted(ds, 0, row, delta, first_pixel, last_pixel, zero, zero)
+                    edges.add(t, delta)
+            left, right = edges.columns()
+            edge_f[72 + 16 * k : 88 + 16 * k, :] = left
+            edge_f[312 + 16 * k : 328 + 16 * k, :] = right
             bias_acc[1] += total
-            return carry
-
-        lax.fori_loop(0, tiles // 2, conv, 0)
+
+        in_turn(dot, after)
         dma_out(s).start()
 
         fold_f[0:96, :] = jnp.zeros((96, C), f32)
@@ -870,105 +890,120 @@
             fold_f[15 + 17 * side : 16 + 17 * side, :] = cells[15:16]
             fold_f[63 + 17 * side : 64 + 17 * side, :] = cells[16 + height : 17 + height]
 
-        def back(c, carry):
-            grad = jnp.dot(pair_window(ds, 0, 28 * c, 14), wback[...], preferred_element_type=f32)
-            rows = split_pairs(grad, C)
-            for t in range(28):
-                ghid[s, 28 * c + t] = rows[t]
-            return carry
-
-        lax.fori_loop(0, 7, back, 0)
-        fold_f[16:32, :] = ghid[s, 0]
-        fold_f[64:80, :] = ghid[s, height + 1]
+        ghid[s] = jnp.dot(
+            pair_window(ds, 0, 0, height // 2 + 1), wback[...], preferred_element_type=f32
+        )
+        fold_f[16:32, :] = ghid[s, 0:16, 0:C]
+        fold_f[64:80, :] = ghid[s, 8 * height : 8 * height + 16, C : 2 * C]
         corner_send[s, 0] = fold_f[0:48, :].astype(bf16)
         corner_send[s, 1] = fold_f[48:96, :].astype(bf16)
         send_outer(s)
 
-        weight_sum(hs, s, ds, 2)
+        turn_pairs(s, ds[0, 2 : 2 + height, 1])
         return carry
 
-    def weight_sum(ref, s, delta_ref, first):
+    def turn_pairs(s, value):
+        v = value.reshape(height // 2, 2, pixels, C)
+        turned[s] = jnp.concatenate(
+            [v[:, e].reshape(8 * height, C) for e in range(2)], axis=1
+        ).T
+
+    def weight_sum(ref, window, samples):
         pairs = height // 2
-        if first == 2:
-            v = delta_ref[0, pl.ds(2, height), :, C : 2 * C]
-        else:
-            v = delta_ref[...]
-        v = v.reshape(pairs, 2, 16, C)
-        lhs = jnp.concatenate([v[:, e].reshape(pairs * 16, C) for e in range(2)], axis=1)
-        for w in range(4):
-            x = ref[s, pl.ds(0, height + 2)].reshape(pairs + 1, 2, 16, 3 * C)
-            rhs = (x[:pairs, w] if w < 2 else x[1:, w - 2]).reshape(pairs * 16, 3 * C)
-            acc[:, w * 3 * C : (w + 1) * 3 * C] += lax.dot_general(
-                lhs, rhs, (((0,), (0,)), ((), ())), preferred_element_type=f32
+        lanes = slice(window[0] * 3 * C, (window[-1] + 1) * 3 * C)
+        if samples[0] == 0:
+            acc[:, lanes] = jnp.zeros((2 * C, 3 * C * len(window)), f32)
+
+        def step(s, carry):
+            v = ref[s].reshape(pairs + 1, 2, 3, pixels, C)
+            parts = []
+            for w in window:
+                x = v[:pairs, w] if w < 2 else v[1:, w - 2]
+                parts += [x[:, b].reshape(pairs * pixels, C) for b in range(3)]
+            acc[:, lanes] += jnp.dot(
+                turned[s], jnp.concatenate(parts, axis=1), preferred_element_type=f32
             )
+            return carry
+
+        lax.fori_loop(samples[0], samples[1], step, 0)
 
     lax.fori_loop(0, batch, stage_two, 0)
 
-    share = 9 * C // peers
-    block = share + 16
-
-    def sum_start(g):
-        for i in range(9):
-            at = i * C
+    share = 3 * C // peers
+    blocks = (share + 16, share, share)
+
+    def sum_start(g, p):
+        block = blocks[p]
+        for b in range(3):
+            at = (3 * p + b) * C
             value = (acc[0:C, at : at + C] + acc[C : 2 * C, at + 3 * C : at + 4 * C]).T.astype(bf16)
             for u in range(C // 16):
-                row = at + 16 * u
-                grad_send[g, row // share, row % share : row % share + 16, :] = value[
+                row = b * C + 16 * u
+                grad_send[g, p, row // share, row % share : row % share + 16, :] = value[
                     16 * u : 16 * u + 16
                 ]
-        bias = jnp.broadcast_to(
-            jnp.sum(bias_acc[g], axis=0, keepdims=True), (16, C)
-        ).astype(bf16)
-        for d in range(peers):
-            grad_send[g, d, share:block, :] = bias
+        if p == 0:
+            bias = jnp.broadcast_to(
+                jnp.sum(bias_acc[g], axis=0, keepdims=True), (16, C)
+            ).astype(bf16)
+            for d in range(peers):
+                grad_send[g, p, d, share:block, :] = bias
         for step in range(1, peers):
             to = (plane + step) % peers
             remote(
-                grad_send.at[g, to], grad_recv.at[g, pl.ds(plane * block, block)],
-                gsend_sem.at[g, 0], grecv_sem.at[g, 0], 4 * n + to // tm_count, to % tm_count,
+                grad_send.at[g, p, to, pl.ds(0, block)],
+                grad_recv.at[g, p, pl.ds(plane * block, block)],
+                gsend_sem.at[g, p, 0], grecv_sem.at[g, p, 0],
+                4 * n + to // tm_count, to % tm_count,
             )
-        grad_recv[g, pl.ds(plane * block, block), :] = grad_send[g, plane]
-
-    def sum_plane(g):
-        finish(grad_recv.at[g], (peers - 1) * block, grecv_sem.at[g, 0])
-        total = grad_recv[g, 0:block, :].astype(f32)
+        grad_recv[g, p, pl.ds(plane * block, block), :] = grad_send[g, p, plane, 0:block, :]
+
+    def sum_plane(g, p):
+        block = blocks[p]
+        finish(grad_recv.at[g, p], (peers - 1) * block, grecv_sem.at[g, p, 0])
+        total = grad_recv[g, p, 0:block, :].astype(f32)
         for d in range(1, peers):
-            total = total + grad_recv[g, d * block : (d + 1) * block, :].astype(f32)
-        plane_send[g] = total.astype(bf16)
+            total = total + grad_recv[g, p, d * block : (d + 1) * block, :].astype(f32)
+        plane_send[g, p, 0:block, :] = total.astype(bf16)
         for step in range(1, 4):
             remote(
-                plane_send.at[g], plane_recv.at[g, pl.ds(n * block, block)],
-                gsend_sem.at[g, 1], grecv_sem.at[g, 1], wrap(me + 4 * step),
+                plane_send.at[g, p, pl.ds(0, block)],
+                plane_recv.at[g, p, pl.ds(n * block, block)],
+                gsend_sem.at[g, p, 1], grecv_sem.at[g, p, 1], wrap(me + 4 * step),
             )
-        plane_recv[g, pl.ds(n * block, block), :] = total.astype(bf16)
-
-    def sum_copies(g, bias_out):
-        finish(plane_recv.at[g], 3 * block, grecv_sem.at[g, 1])
-        total = plane_recv[g, 0:block, :].astype(f32)
+        plane_recv[g, p, pl.ds(n * block, block), :] = total.astype(bf16)
+
+    def sum_copies(g, p):
+        block = blocks[p]
+        finish(plane_recv.at[g, p], 3 * block, grecv_sem.at[g, p, 1])
+        total = plane_recv[g, p, 0:block, :].astype(f32)
         for d in range(1, 4):
-            total = total + plane_recv[g, d * block : (d + 1) * block, :].astype(f32)
+            total = total + plane_recv[g, p, d * block : (d + 1) * block, :].astype(f32)
         pixel_count = 16 * height * pixels * batch * tm_count
         total = total * (1.0 / math.sqrt(pixel_count))
-        bias_out[...] = total[share : share + 1]
+        if p == 0:
+            (gb1_ref, gb2_ref)[g][...] = total[share : share + 1]
         mine = total[0:share].astype(bf16)
-        part_send[g] = mine
+        part_send[g, p] = mine
         for step in range(1, peers):
             to = (plane + step) % peers
             remote(
-                part_send.at[g], part_recv.at[g, pl.ds(plane * share, share)],
-                gsend_sem.at[g, 2], grecv_sem.at[g, 2], 4 * n + to // tm_count, to % tm_count,
+                part_send.at[g, p], part_recv.at[g, p, pl.ds(plane * share, share)],
+                gsend_sem.at[g, p, 2], grecv_sem.at[g, p, 2],
+                4 * n + to // tm_count, to % tm_count,
             )
-        part_recv[g, pl.ds(plane * share, share), :] = mine
-
-    def sum_end(g, weight_out):
-        finish(part_recv.at[g], (peers - 1) * share, grecv_sem.at[g, 2])
-        weight_out[...] = part_recv[g].astype(f32)
-        finish(grad_recv.at[g], (peers - 1) * block, gsend_sem.at[g, 0])
-        finish(plane_recv.at[g], 3 * block, gsend_sem.at[g, 1])
-        finish(part_recv.at[g], (peers - 1) * share, gsend_sem.at[g, 2])
-
-    sum_start(1)
-    acc[...] = jnp.zeros_like(acc)
+        part_recv[g, p, pl.ds(plane * share, share), :] = mine
+
+    def sum_end(g, p):
+        finish(part_recv.at[g, p], (peers - 1) * share, grecv_sem.at[g, p, 2])
+        (gw1_ref, gw2_ref)[g][3 * C * p : 3 * C * (p + 1), :] = part_recv[g, p].astype(f32)
+
+    weight_sum(hs, (0, 1), (0, batch))
+    sum_start(1, 0)
+    weight_sum(hs, (2,), (0, batch))
+    sum_start(1, 1)
+    weight_sum(hs, (3,), (0, batch))
+    sum_start(1, 2)
 
     def stage_three(s, carry):
         @pl.when((j == 0) | (j == 3))
@@ -1019,8 +1054,8 @@
             last = right_at + height - 1
             fold_f[last : last + 1, :] += corner[0:1]
 
-        ghid[s, 1] += outer_recv[s, 2 * height : 2 * height + 16, :].astype(f32)
-        ghid[s, height] += outer_recv[s, 2 * height + 16 : 2 * height + 32, :].astype(f32)
+        ghid[s, 0:16, C : 2 * C] += outer_recv[s, 2 * height : 2 * height + 16, :].astype(f32)
+        ghid[s, 8 * height : 8 * height + 16, 0:C] += outer_recv[s, 2 * height + 16 : 2 * height + 32, :].astype(f32)
 
         def scale(k, carry):
             total = jnp.zeros((pixels, C), f32)
@@ -1030,7 +1065,8 @@
                     left = fold_f[pl.ds(left_at + 16 * k + t, 8), :]
                     right = fold_f[pl.ds(right_at + 16 * k + t, 8), :]
                 at = t % 8
-                value = ghid[s, 1 + 16 * k + t]
+                pair, e = (1 + t) // 2, (1 + t) % 2
+                value = ghid[s, pl.ds(128 * k + 16 * pair, 16), e * C : (e + 1) * C]
                 low = value[:8] + jnp.where(half == 0, turned_by(left, -at), 0.0)
                 high = value[8:] + jnp.where(half == 7, turned_by(right, 7 - at), 0.0)
                 delta = jnp.concatenate([low, high], axis=0) * slope[s, 16 * k + t]
@@ -1040,21 +1076,27 @@
             return carry
 
         lax.fori_loop(0, tiles, scale, 0)
-        weight_sum(xs, s, d1, 0)
-
-        @pl.when(s == 0)
-        def _():
-            sum_plane(1)
-
-        @pl.when(s == min(1, batch - 1))
-        def _():
-            sum_copies(1, gb2_ref)
-
+        turn_pairs(s, d1[...])
         return carry
 
-    lax.fori_loop(0, batch, stage_three, 0)
-    sum_start(0)
-    sum_end(1, gw2_ref)
+    middle = batch // 2
+    lax.fori_loop(0, middle, stage_three, 0)
+    sum_plane(1, 0)
+    lax.fori_loop(middle, batch, stage_three, 0)
+    sum_plane(1, 1)
+    weight_sum(xs, (0, 1), (0, middle))
+    sum_plane(1, 2)
+    sum_copies(1, 0)
+    weight_sum(xs, (0, 1), (middle, batch))
+    sum_start(0, 0)
+    sum_copies(1, 1)
+    weight_sum(xs, (2,), (0, batch))
+    sum_start(0, 1)
+    sum_copies(1, 2)
+    weight_sum(xs, (3,), (0, middle))
+    sum_plane(0, 0)
+    weight_sum(xs, (3,), (middle, batch))
+    sum_start(0, 2)
 
     for s in range(batch):
         dma_out(s).wait()
@@ -1069,9 +1111,47 @@
             finish(all_rows, 416, send_sem.at[1, s])
             finish(all_rows, 480, osend_sem.at[s])
 
-    sum_plane(0)
-    sum_copies(0, gb1_ref)
-    sum_end(0, gw1_ref)
+    for p in range(3):
+        sum_end(1, p)
+    sum_plane(0, 1)
+    sum_copies(0, 0)
+    sum_plane(0, 2)
+    sum_copies(0, 1)
+    sum_end(0, 0)
+    sum_copies(0, 2)
+    sum_end(0, 1)
+    sum_end(0, 2)
+    for g in range(2):
+        for p in range(3):
+            finish(grad_recv.at[g, p], (peers - 1) * blocks[p], gsend_sem.at[g, p, 0])
+            finish(plane_recv.at[g, p], 3 * blocks[p], gsend_sem.at[g, p, 1])
+            finish(part_recv.at[g, p], (peers - 1) * share, gsend_sem.at[g, p, 2])
+
+
+def hand_over(*refs):
+    sources, targets, held, sems = refs[:5], refs[5:10], refs[10:15], refs[15]
+    parts = 4
+    views = []
+    tiles = sources[0].shape[0] // parts
+    for i in range(parts):
+        views.append(tuple(r[0].at[pl.ds(i * tiles, tiles)] for r in (sources, held, targets)))
+    for i in range(1, 5):
+        views.append((sources[i], held[i], targets[i]))
+    arriving = [
+        pltpu.make_async_copy(source, middle, sems.at[0, i])
+        for i, (source, middle, _) in enumerate(views)
+    ]
+    leaving = [
+        pltpu.make_async_copy(middle, target, sems.at[1, i])
+        for i, (_, middle, target) in enumerate(views)
+    ]
+    for copy in arriving:
+        copy.start()
+    for first, second in zip(arriving, leaving):
+        first.wait()
+        second.start()
+    for copy in leaving:
+        copy.wait()
 
 
 def strip_body(features, weight_one, bias_one, weight_two, bias_two, cotangent):
@@ -1080,7 +1160,7 @@
     height = tiles * pixels
     bf16, f32 = jnp.bfloat16, jnp.float32
     peers = 4 * tm_count
-    share = 9 * C // peers
+    share = 3 * C // peers
     block = share + 16
     vmem = pl.BlockSpec(memory_space=pltpu.VMEM)
     hbm = pl.BlockSpec(memory_space=pl.ANY)
@@ -1097,12 +1177,14 @@
         ],
         scratch_shapes=[
             pltpu.VMEM(features.shape, bf16),
-            pltpu.VMEM((batch, height + 2, pixels, 3 * C), bf16),
-            pltpu.VMEM((batch, height + 2, pixels, 3 * C), bf16),
-            pltpu.VMEM((1, height + 6, pixels, 3 * C), bf16),
+            pltpu.VMEM((batch, height + 2, 3, pixels, C), bf16),
+            pltpu.VMEM((batch, height + 2, 3, pixels, C), bf16),
+            pltpu.VMEM((1, height + 4, 3, pixels, C), bf16),
             pltpu.VMEM((height, pixels, C), bf16),
+            pltpu.VMEM((batch, 2 * C, 8 * height), bf16),
             pltpu.VMEM((batch, height, pixels, C), f32),
-            pltpu.VMEM((batch, height + 4, pixels, C), f32),
+            pltpu.VMEM((batch, 8 * height + 16, 2 * C), f32),
+            pltpu.VMEM((8 * height, 2 * C), f32),
             pltpu.VMEM((12 * C, 2 * C), bf16),
             pltpu.VMEM((12 * C, 2 * C), bf16),
             pltpu.VMEM((12 * C, 2 * C), bf16),
@@ -1116,14 +1198,14 @@
             pltpu.VMEM((batch, 2, height + 32, C), bf16),
             pltpu.VMEM((batch, 2, 48, C), bf16),
             pltpu.VMEM((batch, 2 * height + 240, C), bf16),
-            pltpu.VMEM((2, peers, block, C), bf16),
-            pltpu.VMEM((2, peers * block, C), bf16),
-            pltpu.VMEM((2, 4 * block, C), bf16),
-            pltpu.VMEM((2, block, C), bf16),
-            pltpu.VMEM((2, share, C), bf16),
-            pltpu.VMEM((2, 9 * C, C), bf16),
+            pltpu.VMEM((2, 3, peers, block, C), bf16),
+            pltpu.VMEM((2, 3, peers * block, C), bf16),
+            pltpu.VMEM((2, 3, 4 * block, C), bf16),
+            pltpu.VMEM((2, 3, block, C), bf16),
+            pltpu.VMEM((2, 3, share, C), bf16),
+            pltpu.VMEM((2, 3, 3 * C, C), bf16),
             dma((batch,)), dma((batch,)), dma((batch,)),
-            dma((2, batch)), dma((2, batch)), dma((batch,)), dma((batch,)), dma((2, 3)), dma((2, 3)),
+            dma((2, batch)), dma((2, batch)), dma((batch,)), dma((batch,)), dma((2, 3, 3)), dma((2, 3, 3)),
         ],
         compiler_params=pltpu.CompilerParams(
             collective_id=0, has_side_effects=True, vmem_limit_bytes=60 * 1024 * 1024
@@ -1135,6 +1217,15 @@
         features, cotangent, weight_one, bias_one.reshape(1, C), weight_two,
         bias_two.reshape(1, C),
     )
+    results = [output, gw1, gb1, gw2, gb2]
+    output, gw1, gb1, gw2, gb2 = pl.pallas_call(
+        hand_over,
+        in_specs=[hbm] * 5,
+        out_specs=[hbm] * 5,
+        out_shape=[jax.ShapeDtypeStruct(r.shape, r.dtype) for r in results],
+        scratch_shapes=[pltpu.VMEM(r.shape, r.dtype) for r in results] + [dma((2, 8))],
+        compiler_params=pltpu.CompilerParams(vmem_limit_bytes=60 * 1024 * 1024),
+    )(*results)
     shape = weight_one.shape
     return (output, gw1.reshape(shape), gb1.reshape(C), gw2.reshape(shape), gb2.reshape(C))
 

time: 103 us -> 82.7 us (0.80)
  Pallas kernels: 94.9 us -> 81.9 us
  local copies, waits for them, and re-layouts: 7.26 us -> 0 us
    pallas_call x1, Pallas kernels: 94.9 us -> 78.3 us  [strip_body(): pl.pallas_call(functools.partial(strip_kernel, tm_count), in_specs=[hbm,...]
    unnamed x13 -> x0, local copies, waits for them, and re-layouts: 7.26 us -> none
    pallas_call x0 -> x1, Pallas kernels: none -> 3.53 us  [strip_body(): pl.pallas_call(hand_over, in_specs=[hbm] * 5, out_specs=[hbm] * 5, out_sh...]
where the time goes in v2:
time: 82.7 us; the launch traced here: 82.5 us
  Pallas kernels  81.9 us (99%)
    pallas_call x1, Pallas kernels, strip_body(): pl.pallas_call(functools.partial(strip_kernel, tm_count), in_specs=[hbm,...  78.3 us
    pallas_call x1, Pallas kernels, strip_body(): pl.pallas_call(hand_over, in_specs=[hbm] * 5, out_specs=[hbm] * 5, out_sh...  3.53 us

profile of v2, /device:TPU:0, one launch (start us, length us, event | category | flops | bytes accessed | tf_op | source)
XLA Modules:
  0.0 82.5 jit_solution(108571586234734947)
XLA Ops:
  0.6 78.3 %shard_map.101 = (bf16[12,4,16,16,128]{4,3,2,1,0:T(8,128)(2,1)}, f32[1152,128]{1,0:T(8,128)}, f32[1,128]{1,0:T(1,128)}, f32[1152,128]{1,0:T(8,128)}, f32[1,128]{1,0:T(1,128)}) custom-call(bf16[12,4,16,16,128]{4,3,2,1,0:T(8,128)(2,1)} %x_hbm.1, bf16[12,4,16,16,128]{4,3,2,1,0:T(8,128)(2,1)} %cot_hbm.1, bf16[3,3,128,128]{3,2,1,0:T(8,128)(2,1)} %w1_ref.1, ...), custom_call_target="tpu_custom_call" | custom-call | flops 18119393280 | bytes 9437184 | tf_op jit(solution)/shard_map/pallas_call | solution.py:1169
  79.0 3.5 %shard_map.102 = (bf16[12,4,16,16,128]{4,3,2,1,0:T(8,128)(2,1)}, f32[1152,128]{1,0:T(8,128)}, f32[1,128]{1,0:T(1,128)}, f32[1152,128]{1,0:T(8,128)}, f32[1,128]{1,0:T(1,128)}) custom-call(bf16[12,4,16,16,128]{4,3,2,1,0:T(8,128)(2,1)} %get-tuple-element.15.refs_0_, f32[1152,128]{1,0:T(8,128)} %get-tuple-element.16.refs_1_, ...), custom_call_target="tpu_custom_call" | custom-call | tf_op jit(solution)/shard_map/pallas_call | solution.py:1221

commit v3 on v2

--- a/solution.py
+++ b/solution.py
@@ -724,17 +724,30 @@
     bias_two = jnp.concatenate([b2_ref[...], b2_ref[...]], axis=1)
     bias_acc[...] = jnp.zeros_like(bias_acc)
 
+    def build_one(s, k):
+        for t in range(16):
+            xs[s, 1 + 16 * k + t, 1] = field[k, s, t]
+        shift_tile(0, s, k, xs, lambda t: field[k, s, t].astype(f32))
+
+    def build_two(s, k):
+        shift_tile(1, s, k, hs, lambda t: hs[s, 1 + 16 * k + t, 1].astype(f32))
+
+    def first_copies(f, ref, build):
+        finish(halo_recv.at[f, 0], 2 * height + 96, recv_sem.at[f, 0])
+        put_halo_rows(f, 0, ref)
+
+        def step(k, carry):
+            build(0, k)
+            return carry
+
+        lax.fori_loop(0, tiles, step, 0)
+
     def stage_one(s, carry):
-        finish(halo_recv.at[0, s], 2 * height + 96, recv_sem.at[0, s])
-        put_halo_rows(0, s, xs)
-
-        def build(k, carry):
-            for t in range(16):
-                xs[s, 1 + 16 * k + t, 1] = field[k, s, t]
-            shift_tile(0, s, k, xs, lambda t: field[k, s, t].astype(f32))
-            return carry
-
-        lax.fori_loop(0, tiles, build, 0)
+        @pl.when(s + 1 < batch)
+        def _():
+            finish(halo_recv.at[0, s + 1], 2 * height + 96, recv_sem.at[0, s + 1])
+
+        following = s + 1 - (s + 1) // batch
 
         def dot(c):
             pre_f[rows_of * c : rows_of * (c + 1), :] = jnp.dot(
@@ -758,7 +771,19 @@
                     edges.add(t, row)
             put_edges(1, s, k, edges)
 
-        in_turn(dot, after)
+        dot(0)
+        put_halo_rows(0, following, xs)
+        for k in range(tiles // 2):
+            build_one(following, k)
+        dot(1)
+        for k in range(tiles // 2, tiles):
+            build_one(following, k)
+            if k % 2:
+                after((k - tiles // 2) // 2)
+        after(3)
+        dot(2)
+        for k in range(4, tiles):
+            after(k)
         put_corners(1, s)
         top = hs.at[s, 1, 1]
         bottom = hs.at[s, height, 1]
@@ -776,17 +801,10 @@
 
     all_rows = outer_recv.at[0]
     chunks = 3
-    per_chunk = height // 2 // chunks
+    per_chunk = pairs_of = height // 2 // chunks
     rows_of = 16 * per_chunk
 
-    def in_turn(dot, after):
-        for c in range(chunks + 1):
-            if c < chunks:
-                dot(c)
-            if c > 0:
-                for k in range(tiles // chunks * (c - 1), tiles // chunks * c):
-                    after(k)
-
+    first_copies(0, xs, build_one)
     lax.fori_loop(0, batch, stage_one, 0)
 
     for at in (0, 1, height + 2, height + 3):
@@ -835,14 +853,12 @@
         remote(bb, cut(land, extra + 48 * j, 48), ss, rs, wrap(4 * n - 1))
 
     def stage_two(s, carry):
-        finish(halo_recv.at[1, s], 2 * height + 96, recv_sem.at[1, s])
-        put_halo_rows(1, s, hs)
-
-        def build(k, carry):
-            shift_tile(1, s, k, hs, lambda t: hs[s, 1 + 16 * k + t, 1].astype(f32))
-            return carry
-
-        lax.fori_loop(0, tiles, build, 0)
+        @pl.when(s + 1 < batch)
+        def _():
+            finish(halo_recv.at[1, s + 1], 2 * height + 96, recv_sem.at[1, s + 1])
+
+        following = s + 1 - (s + 1) // batch
+        earlier = s - (s + batch - 1) // batch
         dma_cot(s).wait()
 
         def dot(c):
@@ -876,7 +892,30 @@
             edge_f[312 + 16 * k : 328 + 16 * k, :] = right
             bias_acc[1] += total
 
-        in_turn(dot, after)
+        def back(c):
+            first, last = (pairs_of * c, pairs_of * (c + 1) + c // (chunks - 1))
+            ghid[s, 16 * first : 16 * last] = jnp.dot(
+                pair_window(ds, 0, 2 * first, last - first), wback[...],
+                preferred_element_type=f32,
+            )
+
+        dot(0)
+        dot(1)
+        for k in range(tiles):
+            after(k)
+            if k == 3:
+                dot(2)
+            if k in (1, 5, 9):
+                window_sum(hs, earlier, s, ((1, 5, 9).index(k),))
+            if k in (6, 10):
+                back((k - 6) // 4)
+        window_sum(hs, earlier, s, (3,))
+        put_halo_rows(1, following, hs)
+        for k in range(tiles // 2):
+            build_two(following, k)
+        back(2)
+        for k in range(tiles // 2, tiles):
+            build_two(following, k)
         dma_out(s).start()
 
         fold_f[0:96, :] = jnp.zeros((96, C), f32)
@@ -890,9 +929,6 @@
             fold_f[15 + 17 * side : 16 + 17 * side, :] = cells[15:16]
             fold_f[63 + 17 * side : 64 + 17 * side, :] = cells[16 + height : 17 + height]
 
-        ghid[s] = jnp.dot(
-            pair_window(ds, 0, 0, height // 2 + 1), wback[...], preferred_element_type=f32
-        )
         fold_f[16:32, :] = ghid[s, 0:16, 0:C]
         fold_f[64:80, :] = ghid[s, 8 * height : 8 * height + 16, C : 2 * C]
         corner_send[s, 0] = fold_f[0:48, :].astype(bf16)
@@ -904,29 +940,36 @@
 
     def turn_pairs(s, value):
         v = value.reshape(height // 2, 2, pixels, C)
-        turned[s] = jnp.concatenate(
+        turned[s + 1] = jnp.concatenate(
             [v[:, e].reshape(8 * height, C) for e in range(2)], axis=1
         ).T
 
+    def window_sum(ref, s, slot, window):
+        pairs = height // 2
+        lanes = slice(window[0] * 3 * C, (window[-1] + 1) * 3 * C)
+        v = ref[s].reshape(pairs + 1, 2, 3, pixels, C)
+        parts = []
+        for w in window:
+            x = v[:pairs, w] if w < 2 else v[1:, w - 2]
+            parts += [x[:, b].reshape(pairs * pixels, C) for b in range(3)]
+        acc[:, lanes] += jnp.dot(
+            turned[slot], jnp.concatenate(parts, axis=1), preferred_element_type=f32
+        )
+
     def weight_sum(ref, window, samples):
-        pairs = height // 2
         lanes = slice(window[0] * 3 * C, (window[-1] + 1) * 3 * C)
         if samples[0] == 0:
             acc[:, lanes] = jnp.zeros((2 * C, 3 * C * len(window)), f32)
 
         def step(s, carry):
-            v = ref[s].reshape(pairs + 1, 2, 3, pixels, C)
-            parts = []
-            for w in window:
-                x = v[:pairs, w] if w < 2 else v[1:, w - 2]
-                parts += [x[:, b].reshape(pairs * pixels, C) for b in range(3)]
-            acc[:, lanes] += jnp.dot(
-                turned[s], jnp.concatenate(parts, axis=1), preferred_element_type=f32
-            )
+            window_sum(ref, s, s + 1, window)
             return carry
 
         lax.fori_loop(samples[0], samples[1], step, 0)
 
+    acc[...] = jnp.zeros_like(acc)
+    turned[0] = jnp.zeros(turned.shape[1:], bf16)
+    first_copies(1, hs, build_two)
     lax.fori_loop(0, batch, stage_two, 0)
 
     share = 3 * C // peers
@@ -998,11 +1041,11 @@
         finish(part_recv.at[g, p], (peers - 1) * share, grecv_sem.at[g, p, 2])
         (gw1_ref, gw2_ref)[g][3 * C * p : 3 * C * (p + 1), :] = part_recv[g, p].astype(f32)
 
-    weight_sum(hs, (0, 1), (0, batch))
+    weight_sum(hs, (0, 1), (batch - 1, batch))
     sum_start(1, 0)
-    weight_sum(hs, (2,), (0, batch))
+    weight_sum(hs, (2,), (batch - 1, batch))
     sum_start(1, 1)
-    weight_sum(hs, (3,), (0, batch))
+    weight_sum(hs, (3,), (batch - 1, batch))
     sum_start(1, 2)
 
     def stage_three(s, carry):
@@ -1080,14 +1123,15 @@
         return carry
 
     middle = batch // 2
-    lax.fori_loop(0, middle, stage_three, 0)
+    most = batch - 1
+    lax.fori_loop(0, most, stage_three, 0)
     sum_plane(1, 0)
-    lax.fori_loop(middle, batch, stage_three, 0)
+    weight_sum(xs, (0, 1), (0, most))
     sum_plane(1, 1)
-    weight_sum(xs, (0, 1), (0, middle))
+    lax.fori_loop(most, batch, stage_three, 0)
     sum_plane(1, 2)
     sum_copies(1, 0)
-    weight_sum(xs, (0, 1), (middle, batch))
+    weight_sum(xs, (0, 1), (most, batch))
     sum_start(0, 0)
     sum_copies(1, 1)
     weight_sum(xs, (2,), (0, batch))
@@ -1181,7 +1225,7 @@
             pltpu.VMEM((batch, height + 2, 3, pixels, C), bf16),
             pltpu.VMEM((1, height + 4, 3, pixels, C), bf16),
             pltpu.VMEM((height, pixels, C), bf16),
-            pltpu.VMEM((batch, 2 * C, 8 * height), bf16),
+            pltpu.VMEM((batch + 1, 2 * C, 8 * height), bf16),
             pltpu.VMEM((batch, height, pixels, C), f32),
             pltpu.VMEM((batch, 8 * height + 16, 2 * C), f32),
             pltpu.VMEM((8 * height, 2 * C), f32),

time: 82.7 us -> 79.7 us (0.964)
  Pallas kernels: 81.9 us -> 78.7 us
    pallas_call x1, Pallas kernels: 78.3 us -> 75.2 us  [strip_body(): pl.pallas_call(functools.partial(strip_kernel, tm_count), in_specs=[hbm,...]
where the time goes in v3:
time: 79.7 us; the launch traced here: 79.5 us
  Pallas kernels  78.7 us (99%)
  between operations  0.8 us (1%)
    pallas_call x1, Pallas kernels, strip_body(): pl.pallas_call(functools.partial(strip_kernel, tm_count), in_specs=[hbm,...  75.2 us
    pallas_call x1, Pallas kernels, strip_body(): pl.pallas_call(hand_over, in_specs=[hbm] * 5, out_specs=[hbm] * 5, out_sh...  3.53 us

profile of v3, /device:TPU:0, one launch (start us, length us, event | category | flops | bytes accessed | tf_op | source)
XLA Modules:
  0.0 79.5 jit_solution(6087217896747032152)
XLA Ops:
  0.6 75.2 %shard_map.101 = (bf16[12,4,16,16,128]{4,3,2,1,0:T(8,128)(2,1)}, f32[1152,128]{1,0:T(8,128)}, f32[1,128]{1,0:T(1,128)}, f32[1152,128]{1,0:T(8,128)}, f32[1,128]{1,0:T(1,128)}) custom-call(bf16[12,4,16,16,128]{4,3,2,1,0:T(8,128)(2,1)} %x_hbm.1, bf16[12,4,16,16,128]{4,3,2,1,0:T(8,128)(2,1)} %cot_hbm.1, bf16[3,3,128,128]{3,2,1,0:T(8,128)(2,1)} %w1_ref.1, ...), custom_call_target="tpu_custom_call" | custom-call | flops 18119393280 | bytes 9437184 | tf_op jit(solution)/shard_map/pallas_call | solution.py:1213
  75.8 3.5 %shard_map.102 = (bf16[12,4,16,16,128]{4,3,2,1,0:T(8,128)(2,1)}, f32[1152,128]{1,0:T(8,128)}, f32[1,128]{1,0:T(1,128)}, f32[1152,128]{1,0:T(8,128)}, f32[1,128]{1,0:T(1,128)}) custom-call(bf16[12,4,16,16,128]{4,3,2,1,0:T(8,128)(2,1)} %get-tuple-element.15.refs_0_, f32[1152,128]{1,0:T(8,128)} %get-tuple-element.16.refs_1_, ...), custom_call_target="tpu_custom_call" | custom-call | tf_op jit(solution)/shard_map/pallas_call | solution.py:1265

commit v4 on v3

--- a/solution.py
+++ b/solution.py
@@ -713,7 +713,7 @@
         wback[(9 if e == 0 else 0) * C + 0 : (12 if e == 0 else 3) * C, e * C : (e + 1) * C] = zeros
     for a in range(3):
         for b in range(3):
-            block = w2_ref[a, b].astype(f32).T.astype(bf16)
+            block = w2_ref[a, b].T
             for e in range(2):
                 at = ((2 + e - a) * 3 + 2 - b) * C
                 wback[at : at + C, e * C : (e + 1) * C] = block
@@ -979,7 +979,8 @@
         block = blocks[p]
         for b in range(3):
             at = (3 * p + b) * C
-            value = (acc[0:C, at : at + C] + acc[C : 2 * C, at + 3 * C : at + 4 * C]).T.astype(bf16)
+            value = acc[0:C, at : at + C] + acc[C : 2 * C, at + 3 * C : at + 4 * C]
+            value = value.astype(bf16).T
             for u in range(C // 16):
                 row = b * C + 16 * u
                 grad_send[g, p, row // share, row % share : row % share + 16, :] = value[
@@ -1100,7 +1101,7 @@
         ghid[s, 0:16, C : 2 * C] += outer_recv[s, 2 * height : 2 * height + 16, :].astype(f32)
         ghid[s, 8 * height : 8 * height + 16, 0:C] += outer_recv[s, 2 * height + 16 : 2 * height + 32, :].astype(f32)
 
-        def scale(k, carry):
+        def scale(k):
             total = jnp.zeros((pixels, C), f32)
             half = lax.broadcasted_iota(jnp.int32, (8, C), 0)
             for t in range(16):
@@ -1116,49 +1117,36 @@
                 d1[16 * k + t] = delta.astype(bf16)
                 total = total + delta
             bias_acc[0] += total
-            return carry
-
-        lax.fori_loop(0, tiles, scale, 0)
+
+        earlier = s - (s + batch - 1) // batch
+        for k in range(tiles):
+            scale(k)
+            if k in (3, 7):
+                window_sum(xs, earlier, s, (k // 4,))
         turn_pairs(s, d1[...])
         return carry
 
     middle = batch // 2
     most = batch - 1
-    lax.fori_loop(0, most, stage_three, 0)
-    sum_plane(1, 0)
-    weight_sum(xs, (0, 1), (0, most))
-    sum_plane(1, 1)
-    lax.fori_loop(most, batch, stage_three, 0)
-    sum_plane(1, 2)
-    sum_copies(1, 0)
-    weight_sum(xs, (0, 1), (most, batch))
+    acc[:, 0 : 6 * C] = jnp.zeros((2 * C, 6 * C), f32)
+    lax.fori_loop(0, batch, stage_three, 0)
+    window_sum(xs, most, batch, (0, 1))
     sum_start(0, 0)
-    sum_copies(1, 1)
+    for p in range(3):
+        sum_plane(1, p)
     weight_sum(xs, (2,), (0, batch))
     sum_start(0, 1)
-    sum_copies(1, 2)
     weight_sum(xs, (3,), (0, middle))
     sum_plane(0, 0)
+    for p in range(3):
+        sum_copies(1, p)
     weight_sum(xs, (3,), (middle, batch))
     sum_start(0, 2)
-
-    for s in range(batch):
-        dma_out(s).wait()
-
-        @pl.when((j == 0) | (j == 3))
-        def _():
-            finish(all_rows, 544, send_sem.at[1, s])
-            finish(all_rows, 496, osend_sem.at[s])
-
-        @pl.when((j != 0) & (j != 3))
-        def _():
-            finish(all_rows, 416, send_sem.at[1, s])
-            finish(all_rows, 480, osend_sem.at[s])
+    sum_plane(0, 1)
+    sum_copies(0, 0)
 
     for p in range(3):
         sum_end(1, p)
-    sum_plane(0, 1)
-    sum_copies(0, 0)
     sum_plane(0, 2)
     sum_copies(0, 1)
     sum_end(0, 0)
@@ -1170,6 +1158,18 @@
             finish(grad_recv.at[g, p], (peers - 1) * blocks[p], gsend_sem.at[g, p, 0])
             finish(plane_recv.at[g, p], 3 * blocks[p], gsend_sem.at[g, p, 1])
             finish(part_recv.at[g, p], (peers - 1) * share, gsend_sem.at[g, p, 2])
+    for s in range(batch):
+        dma_out(s).wait()
+
+        @pl.when((j == 0) | (j == 3))
+        def _():
+            finish(all_rows, 544, send_sem.at[1, s])
+            finish(all_rows, 496, osend_sem.at[s])
+
+        @pl.when((j != 0) & (j != 3))
+        def _():
+            finish(all_rows, 416, send_sem.at[1, s])
+            finish(all_rows, 480, osend_sem.at[s])
 
 
 def hand_over(*refs):

time: 79.7 us -> 79.7 us (level)
  no operation moved by 1% of the time
where the time goes in v4:
time: 79.7 us; the launch traced here: 79.5 us
  Pallas kernels  78.7 us (99%)
  between operations  0.8 us (1%)
    pallas_call x1, Pallas kernels, strip_body(): pl.pallas_call(functools.partial(strip_kernel, tm_count), in_specs=[hbm,...  75.2 us
    pallas_call x1, Pallas kernels, strip_body(): pl.pallas_call(hand_over, in_specs=[hbm] * 5, out_specs=[hbm] * 5, out_sh...  3.53 us

profile of v4, /device:TPU:0, one launch (start us, length us, event | category | flops | bytes accessed | tf_op | source)
XLA Modules:
  0.0 79.5 jit_solution(10103654415495745977)
XLA Ops:
  0.6 75.2 %shard_map.101 = (bf16[12,4,16,16,128]{4,3,2,1,0:T(8,128)(2,1)}, f32[1152,128]{1,0:T(8,128)}, f32[1,128]{1,0:T(1,128)}, f32[1152,128]{1,0:T(8,128)}, f32[1,128]{1,0:T(1,128)}) custom-call(bf16[12,4,16,16,128]{4,3,2,1,0:T(8,128)(2,1)} %x_hbm.1, bf16[12,4,16,16,128]{4,3,2,1,0:T(8,128)(2,1)} %cot_hbm.1, bf16[3,3,128,128]{3,2,1,0:T(8,128)(2,1)} %w1_ref.1, ...), custom_call_target="tpu_custom_call" | custom-call | flops 18119393280 | bytes 9437184 | tf_op jit(solution)/shard_map/pallas_call | solution.py:1213
  75.8 3.5 %shard_map.102 = (bf16[12,4,16,16,128]{4,3,2,1,0:T(8,128)(2,1)}, f32[1152,128]{1,0:T(8,128)}, f32[1,128]{1,0:T(1,128)}, f32[1152,128]{1,0:T(8,128)}, f32[1,128]{1,0:T(1,128)}) custom-call(bf16[12,4,16,16,128]{4,3,2,1,0:T(8,128)(2,1)} %get-tuple-element.15.refs_0_, f32[1152,128]{1,0:T(8,128)} %get-tuple-element.16.refs_1_, ...), custom_call_target="tpu_custom_call" | custom-call | tf_op jit(solution)/shard_map/pallas_call | solution.py:1265
